TPU v7x, 256 devices: a whole 4x4x8 slice. The times are simulated.
256 devices in a mesh: seq: 32 (over z, x_lo, core), head: 8 (over x_hi, y).
Axes of the slice: x: 4 (x_hi: 2, x_lo: 2; x = x_hi * 2 + x_lo), y: 4, z: 8, core: 2. Of those that a mesh axis runs over, the one named last changes fastest.
Arguments:
- queries: bfloat16 [8192, 2048], P('seq', 'head'), may hold values from -6 to 6
- key_vectors: bfloat16 [8192, 2048], P('seq', 'head'), may hold values from -6 to 6
- value_vectors: bfloat16 [8192, 2048], P('seq', 'head'), may hold values from -3 to 3
- group_order: int32 [64], replicated, may hold values from 0 to 63, each once
- doc_lengths: int32 [8], replicated, may hold values from 1 to 3072, 8192 in all
- out_grad: bfloat16 [8192, 4096], P('seq'), may hold values from -2.09375 to 2.09375
- out_weight: bfloat16 [2048, 4096], P('head'), may hold values from -0.125 to 0.125
Outputs:
- layer_out: bfloat16 [8192, 4096], P('seq', 'head')
- grad_queries: bfloat16 [8192, 2048], P('seq', 'head')
- grad_keys: bfloat16 [8192, 2048], P('seq', 'head')
- grad_values: bfloat16 [8192, 2048], P('seq', 'head')
Inputs may be any that keep to these rules, and one draw needn't show every extreme that they name: `group_order`: every group number appears exactly once. `doc_lengths`: the lengths sum to 8192; the longest is exactly 3072.
All inputs are finite; a program needn't handle non-finite values.
Results may differ from a plain program's by a relative error of at most 0.03.
Values may be sent and summed in bfloat16 or wider, within the bound.
A program may use at most 128 MiB of HBM per device.

v0:
```python
import math

import jax
import jax.numpy as jnp
from jax import lax
from jax.sharding import PartitionSpec as P

HD = 128


EXCLUDED = -1e30


def from_behind(block, axis, distance):
    devices = range(lax.axis_size(axis))
    route = [((i - distance) % len(devices), i) for i in devices]
    return lax.ppermute(block, axis, route)


def group_lookup(row_ids, group_order, half_group):
    slot_ids = row_ids // half_group
    slot_match = slot_ids[:, None] == jnp.arange(group_order.shape[0], dtype=jnp.int32)[None, :]
    chosen = jnp.sum(jnp.where(slot_match, group_order[None, :], 0), axis=1)
    return chosen * half_group + row_ids % half_group


def document_index(placed, doc_lengths):
    doc_ends = jnp.cumsum(doc_lengths)
    return jnp.sum((placed[:, None] >= doc_ends[None, :]).astype(jnp.int32), axis=1)


def visible_pairs(query_pos, query_doc, key_pos, key_doc):
    return (key_pos[None, :] <= query_pos[:, None]) & (key_doc[None, :] == query_doc[:, None])


def per_device(queries, key_vectors, value_vectors, group_order, doc_lengths, out_grad, out_weight):
    tok_rows = queries.shape[0]
    heads_here = queries.shape[1] // HD
    half_group = tok_rows // 2
    score_scale = 1.0 / math.sqrt(HD)
    cycle_size = lax.axis_size("seq")
    my_rank = lax.axis_index("seq")

    def locate(first_row, row_count):
        row_ids = first_row + jnp.arange(row_count, dtype=jnp.int32)
        placed = group_lookup(row_ids, group_order, half_group)
        return (placed, document_index(placed, doc_lengths))

    own_pos, own_doc = locate(my_rank * tok_rows, tok_rows)
    query_heads = queries.reshape(tok_rows, heads_here, HD)
    key_heads = key_vectors.reshape(tok_rows, heads_here, HD)
    value_heads = value_vectors.reshape(tok_rows, heads_here, HD)
    arrived = (
        lax.all_gather(key_vectors, "seq", axis=0, tiled=True),
        lax.all_gather(value_vectors, "seq", axis=0, tiled=True),
    )
    row_max = jnp.full((heads_here, tok_rows), EXCLUDED, jnp.float32)
    summed = jnp.zeros((tok_rows, heads_here, HD), jnp.float32)
    row_count = arrived[0].shape[0]
    key_part = arrived[0].reshape(row_count, heads_here, HD)
    value_part = arrived[1].reshape(row_count, heads_here, HD)
    key_pos, key_doc = locate(jnp.int32(0), row_count)
    visible = visible_pairs(own_pos, own_doc, key_pos, key_doc)
    logits = (
        jnp.einsum("qhd,khd->hqk", query_heads, key_part, preferred_element_type=jnp.float32)
        * score_scale
    )
    logits = jnp.where(visible[None], logits, EXCLUDED)
    new_max = jnp.maximum(row_max, jnp.max(logits, axis=2))
    weights = jnp.where(visible[None], jnp.exp(logits - new_max[:, :, None]), 0.0)
    factor = jnp.exp(row_max - new_max)
    new_totals = jnp.sum(weights, axis=2)
    product = jnp.einsum(
        "hqk,khd->qhd", weights.astype(jnp.bfloat16), value_part, preferred_element_type=jnp.float32
    )
    row_max, totals, summed = (new_max, new_totals, summed * factor.T[:, :, None] + product)
    log_total = row_max + jnp.log(totals)
    attention = (summed / totals.T[:, :, None]).astype(jnp.bfloat16)
    partial_value = jnp.dot(
        attention.reshape(tok_rows, heads_here * HD), out_weight, preferred_element_type=jnp.float32
    )
    layer_out = lax.psum_scatter(partial_value, "head", scatter_dimension=1, tiled=True).astype(
        jnp.bfloat16
    )
    d_attention = lax.dot_general(
        out_grad, out_weight, (((1,), (1,)), ((), ())), preferred_element_type=jnp.float32
    ).astype(jnp.bfloat16)
    grad_heads = d_attention.reshape(tok_rows, heads_here, HD)
    row_delta = jnp.einsum(
        "qhd,qhd->hq", grad_heads.astype(jnp.float32), attention.astype(jnp.float32)
    )

    def tile_grads(
        query_block,
        grad_block,
        log_block,
        delta_block,
        query_pos,
        query_doc,
        key_local,
        value_local,
    ):
        visible = visible_pairs(query_pos, query_doc, own_pos, own_doc)
        logits = (
            jnp.einsum("qhd,khd->hqk", query_block, key_local, preferred_element_type=jnp.float32)
            * score_scale
        )
        logits = jnp.where(visible[None], logits, EXCLUDED)
        probs_full = jnp.where(visible[None], jnp.exp(logits - log_block[:, :, None]), 0.0)
        value_term = jnp.einsum(
            "hqk,qhd->khd",
            probs_full.astype(jnp.bfloat16),
            grad_block,
            preferred_element_type=jnp.float32,
        )
        dprobs = jnp.einsum(
            "qhd,khd->hqk", grad_block, value_local, preferred_element_type=jnp.float32
        )
        dscores = (probs_full * (dprobs - delta_block[:, :, None]) * score_scale).astype(
            jnp.bfloat16
        )
        query_term = jnp.einsum(
            "hqk,khd->qhd", dscores, key_local, preferred_element_type=jnp.float32
        )
        key_term = jnp.einsum(
            "hqk,qhd->khd", dscores, query_block, preferred_element_type=jnp.float32
        )
        return (query_term, key_term, value_term)

    def accumulate(
        step_index,
        sign,
        query_block,
        grad_block,
        query_grads,
        log_block,
        delta_block,
        key_local,
        value_local,
    ):
        owner_rank = (my_rank - sign * step_index) % cycle_size
        query_pos, query_doc = locate(owner_rank * tok_rows, tok_rows)
        query_term, key_term, value_term = tile_grads(
            query_block,
            grad_block,
            log_block,
            delta_block,
            query_pos,
            query_doc,
            key_local,
            value_local,
        )
        return (query_grads + query_term, key_term, value_term)

    zero_grads = jnp.zeros((tok_rows, heads_here, HD), jnp.float32)

    def cycle_step(step_index, cycle_state):
        query_block, grad_block, query_acc, log_block, delta_block, key_grads, value_grads = (
            cycle_state
        )
        query_acc, key_term, value_term = accumulate(
            step_index,
            1,
            query_block,
            grad_block,
            query_acc,
            log_block,
            delta_block,
            key_heads,
            value_heads,
        )
        query_block, grad_block = from_behind((query_block, grad_block), "seq", 1)
        query_acc, log_block, delta_block = from_behind(
            (query_acc, log_block, delta_block), "seq", 1
        )
        return (
            query_block,
            grad_block,
            query_acc,
            log_block,
            delta_block,
            key_grads + key_term,
            value_grads + value_term,
        )

    start_cycle = (
        query_heads,
        grad_heads,
        zero_grads,
        log_total,
        row_delta,
        zero_grads,
        zero_grads,
    )
    query_block, grad_block, query_acc, log_block, delta_block, key_grads, value_grads = (
        lax.fori_loop(0, cycle_size - 1, cycle_step, start_cycle)
    )
    query_acc, key_term, value_term = accumulate(
        cycle_size - 1,
        1,
        query_block,
        grad_block,
        query_acc,
        log_block,
        delta_block,
        key_heads,
        value_heads,
    )
    key_grads = key_grads + key_term
    value_grads = value_grads + value_term
    query_grads = from_behind(query_acc, "seq", 1)
    grad_queries = query_grads.reshape(tok_rows, heads_here * HD).astype(jnp.bfloat16)
    grad_keys = key_grads.reshape(tok_rows, heads_here * HD).astype(jnp.bfloat16)
    grad_values = value_grads.reshape(tok_rows, heads_here * HD).astype(jnp.bfloat16)
    return (layer_out, grad_queries, grad_keys, grad_values)


def solution(mesh):
    return jax.shard_map(
        per_device,
        mesh=mesh,
        in_specs=(
            P("seq", "head"),
            P("seq", "head"),
            P("seq", "head"),
            P(),
            P(),
            P("seq", None),
            P("head", None),
        ),
        out_specs=(P("seq", "head"), P("seq", "head"), P("seq", "head"), P("seq", "head")),
        check_vma=False,
    )
```

profile of v0, /device:TPU:1, one launch (start us, length us, event | category | flops | bytes accessed | tf_op | source)
XLA Modules:
  0.0 760.4 jit_solution(5360085561794024247)
XLA Ops:
  23.3 3.4 compare_and_fusion.1
  26.7 60.1 %all-gather.3.cloned.1.call-done = bf16[8192,256]{0,1:T(8,128)(2,1)} async-done(((bf16[256,256]{0,1:T(8,128)(2,1)}), bf16[8192,256]{0,1:T(8,128)(2,1)}) %all-gather.3.cloned.1.call-update) | async-done | bytes 4194320 | tf_op jit(solution)/shard_map/all_gather | solution.py:54
  86.9 6.5 fusion.13
  93.4 5.3 fusion.14
  99.1 55.1 %all-gather.5.cloned.1.call-done = bf16[8192,256]{1,0:T(8,128)(2,1)} async-done(((bf16[256,256]{1,0:T(8,128)(2,1)}), bf16[8192,256]{1,0:T(8,128)(2,1)}) %all-gather.5.cloned.1.call-update) | async-done | bytes 4194320 | tf_op jit(solution)/shard_map/all_gather | solution.py:55
  154.2 6.4 copy.51
  160.6 10.7 %fusion.43 = (f32[2,256]{1,0:T(2,128)S(1)}, bf16[256,2,128]{0,2,1:T(8,128)(2,1)S(1)}) fusion(bf16[256,256]{0,1:T(8,128)(2,1)S(1)} %convolution_convert_fusion, f32[256,2]{0,1:T(2,128)S(1)} %bitcast.121, bf16[8192,2,128]{0,2,1:T(8,128)(2,1)} %bitcast.108, f32[2,256,8192]{2,1,0:T(8,128)} %copy-done.1, f32[2,256]{1,0:T(2,128)S(1)} %broadcast_maximum_fusion, ...), kind=kOutput, calls=%fused_computation.62 | convolution fusion | flops 1095171584 | bytes 23339008 | tf_op jit(solution)/shard_map/hqk,khd->qhd/dot_general | solution.py:73
  174.0 564.4 %while.29 = (s32[]{:T(128)}, bf16[256,2,128]{2,0,1:T(8,128)(2,1)}, bf16[256,2,128]{2,0,1:T(8,128)(2,1)S(1)}, f32[256,2,128]{2,0,1:T(8,128)S(1)}, f32[2,256]{1,0:...) while((s32[]{:T(128)}, bf16[256,2,128]{2,0,1:T(8,128)(2,1)}, ...), condition=%wide.region_11.12_spmd.clone, body=%wide.region_8.11_spmd.clone.sunk | while | flops 169538576 | bytes 7642933 | solution.py:196
  187.9 5.7 collective-permute-done.2
  270.6 6.4 collective-permute-start.4
  340.8 3.0 collective-permute-start.3
  377.2 3.0 collective-permute-start.3
  394.5 3.0 collective-permute-start.3
  414.4 3.0 collective-permute-start.3
  432.2 3.1 collective-permute-start.1
  435.9 3.0 collective-permute-start.3
  485.4 3.0 collective-permute-start.3
  521.7 3.0 collective-permute-start.3
  539.0 3.0 collective-permute-start.3
  558.9 3.0 collective-permute-start.3
  576.8 3.1 collective-permute-start.1
  580.4 3.0 collective-permute-start.3
  721.3 3.1 collective-permute-start.1
  725.0 3.0 collective-permute-start.3
  (786 shorter events, 542.7 us)
Async XLA Ops:
  7.2 79.7 %all-gather.3.cloned.1.call-start = ((), (), s32[]{:S(2)}) async-start(), calls=%async_computation.1 | async-start | bytes 4325376 | tf_op jit(solution)/shard_map/all_gather | solution.py:54
  9.1 145.1 %all-gather.5.cloned.1.call-start = ((), (), s32[]{:S(2)}) async-start(), calls=%async_computation.2 | async-start | bytes 4325376 | tf_op jit(solution)/shard_map/all_gather | solution.py:55
  9.8 742.3 %reduce-scatter.2.cloned.1.call-start = ((), (), s32[]{:S(2)}) async-start(), calls=%async_computation.3 | async-start | bytes 4718592 | tf_op jit(solution)/shard_map/reduce_scatter | solution.py:82
  194.5 16.9 %collective-permute-start = (bf16[256,2,128]{2,0,1:T(8,128)(2,1)S(1)}, bf16[256,2,128]{2,0,1:T(8,128)(2,1)}, u32[]{:S(2)}, u32[]{:S(2)}) collective-permute-start(bf16[256,2,128]{2,0,1:T(8,128)(2,1)S(1)} %copy.94), channel_id=1, source_target_pairs={{248,0},{0,8},{8,16},{16,24},{24,32},{32,40},{40,48},{48,56},{56,6... | collective-permute-start | bytes 393224 | tf_op jit(solution)/shard_map/while/body/eval_jaxpr/ppermute | solution.py:17
  267.6 22.1 %collective-permute-start = (bf16[256,2,128]{2,0,1:T(8,128)(2,1)S(1)}, bf16[256,2,128]{2,0,1:T(8,128)(2,1)}, u32[]{:S(2)}, u32[]{:S(2)}) collective-permute-start(bf16[256,2,128]{2,0,1:T(8,128)(2,1)S(1)} %copy.94), channel_id=1, source_target_pairs={{248,0},{0,8},{8,16},{16,24},{24,32},{32,40},{40,48},{48,56},{56,6... | collective-permute-start | bytes 393224 | tf_op jit(solution)/shard_map/while/body/eval_jaxpr/ppermute | solution.py:17
  270.0 19.7 %collective-permute-start.1 = (bf16[256,2,128]{2,0,1:T(8,128)(2,1)S(1)}, bf16[256,2,128]{2,0,1:T(8,128)(2,1)S(1)}, u32[]{:S(2)}, u32[]{:S(2)}) collective-permute-start(bf16[256,2,128]{2,0,1:T(8,128)(2,1)S(1)} %copy.95), channel_id=1, source_target_pairs={{248,0},{0,8},{8,16},{16,24},{24,32},{32,40},{40,48},{48,56},{56,6... | collective-permute-start | bytes 393224 | tf_op jit(solution)/shard_map/while/body/eval_jaxpr/ppermute | solution.py:17
  270.6 19.1 %collective-permute-start.3 = (f32[2,256]{1,0:T(2,128)}, f32[2,256]{1,0:T(2,128)S(1)}, u32[]{:S(2)}, u32[]{:S(2)}) collective-permute-start(f32[2,256]{1,0:T(2,128)} %copy.97), channel_id=1, source_target_pairs={{248,0},{0,8},{8,16},{16,24},{24,32},{32,40},{40,48},{48,56},{56,6... | collective-permute-start | bytes 6152 | tf_op jit(solution)/shard_map/while/body/eval_jaxpr/ppermute | solution.py:17
  270.6 19.1 %collective-permute-start.4 = (f32[2,256]{1,0:T(2,128)S(1)}, f32[2,256]{1,0:T(2,128)S(1)}, u32[]{:S(2)}, u32[]{:S(2)}) collective-permute-start(f32[2,256]{1,0:T(2,128)S(1)} %copy.98), channel_id=1, source_target_pairs={{248,0},{0,8},{8,16},{16,24},{24,32},{32,40},{40,48},{48,56},{56,6... | collective-permute-start | bytes 6152 | tf_op jit(solution)/shard_map/while/body/eval_jaxpr/ppermute | solution.py:17
  336.1 18.0 %collective-permute-start = (bf16[256,2,128]{2,0,1:T(8,128)(2,1)S(1)}, bf16[256,2,128]{2,0,1:T(8,128)(2,1)}, u32[]{:S(2)}, u32[]{:S(2)}) collective-permute-start(bf16[256,2,128]{2,0,1:T(8,128)(2,1)S(1)} %copy.94), channel_id=1, source_target_pairs={{248,0},{0,8},{8,16},{16,24},{24,32},{32,40},{40,48},{48,56},{56,6... | collective-permute-start | bytes 393224 | tf_op jit(solution)/shard_map/while/body/eval_jaxpr/ppermute | solution.py:17
  372.1 18.4 %collective-permute-start = (bf16[256,2,128]{2,0,1:T(8,128)(2,1)S(1)}, bf16[256,2,128]{2,0,1:T(8,128)(2,1)}, u32[]{:S(2)}, u32[]{:S(2)}) collective-permute-start(bf16[256,2,128]{2,0,1:T(8,128)(2,1)S(1)} %copy.94), channel_id=1, source_target_pairs={{248,0},{0,8},{8,16},{16,24},{24,32},{32,40},{40,48},{48,56},{56,6... | collective-permute-start | bytes 393224 | tf_op jit(solution)/shard_map/while/body/eval_jaxpr/ppermute | solution.py:17
  408.8 19.6 %collective-permute-start = (bf16[256,2,128]{2,0,1:T(8,128)(2,1)S(1)}, bf16[256,2,128]{2,0,1:T(8,128)(2,1)}, u32[]{:S(2)}, u32[]{:S(2)}) collective-permute-start(bf16[256,2,128]{2,0,1:T(8,128)(2,1)S(1)} %copy.94), channel_id=1, source_target_pairs={{248,0},{0,8},{8,16},{16,24},{24,32},{32,40},{40,48},{48,56},{56,6... | collective-permute-start | bytes 393224 | tf_op jit(solution)/shard_map/while/body/eval_jaxpr/ppermute | solution.py:17
  410.8 17.5 %collective-permute-start.1 = (bf16[256,2,128]{2,0,1:T(8,128)(2,1)S(1)}, bf16[256,2,128]{2,0,1:T(8,128)(2,1)S(1)}, u32[]{:S(2)}, u32[]{:S(2)}) collective-permute-start(bf16[256,2,128]{2,0,1:T(8,128)(2,1)S(1)} %copy.95), channel_id=1, source_target_pairs={{248,0},{0,8},{8,16},{16,24},{24,32},{32,40},{40,48},{48,56},{56,6... | collective-permute-start | bytes 393224 | tf_op jit(solution)/shard_map/while/body/eval_jaxpr/ppermute | solution.py:17
  429.3 19.9 %collective-permute-start = (bf16[256,2,128]{2,0,1:T(8,128)(2,1)S(1)}, bf16[256,2,128]{2,0,1:T(8,128)(2,1)}, u32[]{:S(2)}, u32[]{:S(2)}) collective-permute-start(bf16[256,2,128]{2,0,1:T(8,128)(2,1)S(1)} %copy.94), channel_id=1, source_target_pairs={{248,0},{0,8},{8,16},{16,24},{24,32},{32,40},{40,48},{48,56},{56,6... | collective-permute-start | bytes 393224 | tf_op jit(solution)/shard_map/while/body/eval_jaxpr/ppermute | solution.py:17
  432.2 17.0 %collective-permute-start.1 = (bf16[256,2,128]{2,0,1:T(8,128)(2,1)S(1)}, bf16[256,2,128]{2,0,1:T(8,128)(2,1)S(1)}, u32[]{:S(2)}, u32[]{:S(2)}) collective-permute-start(bf16[256,2,128]{2,0,1:T(8,128)(2,1)S(1)} %copy.95), channel_id=1, source_target_pairs={{248,0},{0,8},{8,16},{16,24},{24,32},{32,40},{40,48},{48,56},{56,6... | collective-permute-start | bytes 393224 | tf_op jit(solution)/shard_map/while/body/eval_jaxpr/ppermute | solution.py:17
  516.6 18.4 %collective-permute-start = (bf16[256,2,128]{2,0,1:T(8,128)(2,1)S(1)}, bf16[256,2,128]{2,0,1:T(8,128)(2,1)}, u32[]{:S(2)}, u32[]{:S(2)}) collective-permute-start(bf16[256,2,128]{2,0,1:T(8,128)(2,1)S(1)} %copy.94), channel_id=1, source_target_pairs={{248,0},{0,8},{8,16},{16,24},{24,32},{32,40},{40,48},{48,56},{56,6... | collective-permute-start | bytes 393224 | tf_op jit(solution)/shard_map/while/body/eval_jaxpr/ppermute | solution.py:17
  553.3 19.6 %collective-permute-start = (bf16[256,2,128]{2,0,1:T(8,128)(2,1)S(1)}, bf16[256,2,128]{2,0,1:T(8,128)(2,1)}, u32[]{:S(2)}, u32[]{:S(2)}) collective-permute-start(bf16[256,2,128]{2,0,1:T(8,128)(2,1)S(1)} %copy.94), channel_id=1, source_target_pairs={{248,0},{0,8},{8,16},{16,24},{24,32},{32,40},{40,48},{48,56},{56,6... | collective-permute-start | bytes 393224 | tf_op jit(solution)/shard_map/while/body/eval_jaxpr/ppermute | solution.py:17
  555.4 17.5 %collective-permute-start.1 = (bf16[256,2,128]{2,0,1:T(8,128)(2,1)S(1)}, bf16[256,2,128]{2,0,1:T(8,128)(2,1)S(1)}, u32[]{:S(2)}, u32[]{:S(2)}) collective-permute-start(bf16[256,2,128]{2,0,1:T(8,128)(2,1)S(1)} %copy.95), channel_id=1, source_target_pairs={{248,0},{0,8},{8,16},{16,24},{24,32},{32,40},{40,48},{48,56},{56,6... | collective-permute-start | bytes 393224 | tf_op jit(solution)/shard_map/while/body/eval_jaxpr/ppermute | solution.py:17
  573.8 19.9 %collective-permute-start = (bf16[256,2,128]{2,0,1:T(8,128)(2,1)S(1)}, bf16[256,2,128]{2,0,1:T(8,128)(2,1)}, u32[]{:S(2)}, u32[]{:S(2)}) collective-permute-start(bf16[256,2,128]{2,0,1:T(8,128)(2,1)S(1)} %copy.94), channel_id=1, source_target_pairs={{248,0},{0,8},{8,16},{16,24},{24,32},{32,40},{40,48},{48,56},{56,6... | collective-permute-start | bytes 393224 | tf_op jit(solution)/shard_map/while/body/eval_jaxpr/ppermute | solution.py:17
  576.8 17.0 %collective-permute-start.1 = (bf16[256,2,128]{2,0,1:T(8,128)(2,1)S(1)}, bf16[256,2,128]{2,0,1:T(8,128)(2,1)S(1)}, u32[]{:S(2)}, u32[]{:S(2)}) collective-permute-start(bf16[256,2,128]{2,0,1:T(8,128)(2,1)S(1)} %copy.95), channel_id=1, source_target_pairs={{248,0},{0,8},{8,16},{16,24},{24,32},{32,40},{40,48},{48,56},{56,6... | collective-permute-start | bytes 393224 | tf_op jit(solution)/shard_map/while/body/eval_jaxpr/ppermute | solution.py:17
  661.2 18.4 %collective-permute-start = (bf16[256,2,128]{2,0,1:T(8,128)(2,1)S(1)}, bf16[256,2,128]{2,0,1:T(8,128)(2,1)}, u32[]{:S(2)}, u32[]{:S(2)}) collective-permute-start(bf16[256,2,128]{2,0,1:T(8,128)(2,1)S(1)} %copy.94), channel_id=1, source_target_pairs={{248,0},{0,8},{8,16},{16,24},{24,32},{32,40},{40,48},{48,56},{56,6... | collective-permute-start | bytes 393224 | tf_op jit(solution)/shard_map/while/body/eval_jaxpr/ppermute | solution.py:17
  697.9 19.6 %collective-permute-start = (bf16[256,2,128]{2,0,1:T(8,128)(2,1)S(1)}, bf16[256,2,128]{2,0,1:T(8,128)(2,1)}, u32[]{:S(2)}, u32[]{:S(2)}) collective-permute-start(bf16[256,2,128]{2,0,1:T(8,128)(2,1)S(1)} %copy.94), channel_id=1, source_target_pairs={{248,0},{0,8},{8,16},{16,24},{24,32},{32,40},{40,48},{48,56},{56,6... | collective-permute-start | bytes 393224 | tf_op jit(solution)/shard_map/while/body/eval_jaxpr/ppermute | solution.py:17
  699.9 17.5 %collective-permute-start.1 = (bf16[256,2,128]{2,0,1:T(8,128)(2,1)S(1)}, bf16[256,2,128]{2,0,1:T(8,128)(2,1)S(1)}, u32[]{:S(2)}, u32[]{:S(2)}) collective-permute-start(bf16[256,2,128]{2,0,1:T(8,128)(2,1)S(1)} %copy.95), channel_id=1, source_target_pairs={{248,0},{0,8},{8,16},{16,24},{24,32},{32,40},{40,48},{48,56},{56,6... | collective-permute-start | bytes 393224 | tf_op jit(solution)/shard_map/while/body/eval_jaxpr/ppermute | solution.py:17
  718.4 19.9 %collective-permute-start = (bf16[256,2,128]{2,0,1:T(8,128)(2,1)S(1)}, bf16[256,2,128]{2,0,1:T(8,128)(2,1)}, u32[]{:S(2)}, u32[]{:S(2)}) collective-permute-start(bf16[256,2,128]{2,0,1:T(8,128)(2,1)S(1)} %copy.94), channel_id=1, source_target_pairs={{248,0},{0,8},{8,16},{16,24},{24,32},{32,40},{40,48},{48,56},{56,6... | collective-permute-start | bytes 393224 | tf_op jit(solution)/shard_map/while/body/eval_jaxpr/ppermute | solution.py:17
  721.3 17.0 %collective-permute-start.1 = (bf16[256,2,128]{2,0,1:T(8,128)(2,1)S(1)}, bf16[256,2,128]{2,0,1:T(8,128)(2,1)S(1)}, u32[]{:S(2)}, u32[]{:S(2)}) collective-permute-start(bf16[256,2,128]{2,0,1:T(8,128)(2,1)S(1)} %copy.95), channel_id=1, source_target_pairs={{248,0},{0,8},{8,16},{16,24},{24,32},{32,40},{40,48},{48,56},{56,6... | collective-permute-start | bytes 393224 | tf_op jit(solution)/shard_map/while/body/eval_jaxpr/ppermute | solution.py:17
  (141 other events, 1612.7 us)
Sparse Core Ops, SparseCore 0:
  10.4 76.4 all-gather.2
  88.7 65.4 all-gather.4
  174.0 107.9 reduce-scatter.1
where the time goes:
time: 767 us; the launch traced here: 760 us
  matrix products  276 us (36%)
  starting transfers between devices  191 us (25%)
  waiting for transfers between devices  126 us (16%)
  other arithmetic  86.4 us (11%)
  local copies, waits for them, and re-layouts  64.5 us (8%)
  between operations  14 us (2%)
    ppermute x156, starting transfers between devices, from_behind(): return lax.ppermute(block, axis, route)  190 us
    dot_general x32, matrix products, tile_grads(): jnp.einsum('hqk,qhd->khd', dscores, query_block, preferred_element_type=j...  60.8 us
    all_gather x1, waiting for transfers between devices, per_device(): lax.all_gather(key_vectors, 'seq', axis=0, tiled=True)  60.1 us
    dot_general x32, matrix products, tile_grads(): jnp.einsum('hqk,qhd->khd', probs_full.astype(jnp.bfloat16), grad_block, p...  59.8 us
    dot_general x32, matrix products, tile_grads(): jnp.einsum('hqk,khd->qhd', dscores, key_local, preferred_element_type=jnp...  58.4 us
    all_gather x1, waiting for transfers between devices, per_device(): lax.all_gather(value_vectors, 'seq', axis=0, tiled=True)  55.1 us
    while x124, local copies, waits for them, and re-layouts  46.2 us
    dot_general x32, matrix products, tile_grads(): jnp.einsum('qhd,khd->hqk', query_block, key_local, preferred_element_type...  38.3 us
  transfers between devices with their start and end apart: 159, of which 6 were waited for; matrix products, arithmetic and copies ran while one was open for 53% of the time, Pallas kernels for 0%

commit v1 on v0

v1 whole, which is shorter than its diff:
```python
import functools
import math

import jax
import jax.numpy as jnp
from jax import lax
from jax.experimental import pallas as pl
from jax.experimental.pallas import tpu as pltpu
from jax.sharding import PartitionSpec as P

HD = 128
GROUP = 128
DOCS = 8
NZ = 8
NK = 8
BLK = 512
HALF = 256
PAIR = 2 * BLK
TILE = 256
SCALE = 1.0 / math.sqrt(HD)
HIDDEN = -1e30
LOWEST = -5e29
F32 = jnp.float32
BF16 = jnp.bfloat16
MESH = pl.DeviceIdType.MESH


def dot_nt(a, b):
    return lax.dot_general(a, b, (((1,), (1,)), ((), ())), preferred_element_type=F32)


def dot_nn(a, b):
    return jnp.dot(a, b, preferred_element_type=F32)


def kernel(
    order, lengths, q_in, k_in, v_in, og_hbm, w_hbm,
    layer_out, dq_out, dk_out, dv_out,
    xk, xv, xq, xg,
    og, wfull, wg, da, da_acc, att, attg,
    first, place, last,
    o_acc, m_acc, l_acc, lse_col, delta_col, dq_acc, dk_acc, dv_acc,
    o_send, o_recv, st_send, st_recv, st_z, st_par, grad_send, grad_recv,
    send_sem, recv_sem, local_sem,
):
    s = lax.axis_index("seq")
    k = lax.axis_index("head")
    core = s % 2
    other = 1 - core
    x = (s // 2) % 2
    z = s // 4
    sibling = s + 1 - 2 * core
    partner = s + 2 - 4 * x
    diagonal = partner + 1 - 2 * core

    def z_peer(e):
        return ((z + e) % NZ) * 4 + s % 4

    def seq_dev(t):
        return (t, k)

    def head_dev(e):
        return (s, (k + e) % NK)

    def weight_dev(e):
        kk = (k + e) % NK
        diff = (kk // 4 - k // 4) * (kk // 4 - k // 4)
        return (s + diff * (2 - 4 * x), kk)

    load_w = pltpu.make_async_copy(w_hbm, wfull, local_sem.at[0])
    load_g = pltpu.make_async_copy(og_hbm, og, local_sem.at[1])
    load_w.start()
    load_g.start()

    barrier = pltpu.get_barrier_semaphore()
    targets = [seq_dev(sibling), seq_dev(partner), seq_dev(diagonal)]
    targets += [seq_dev(z_peer(e)) for e in range(1, NZ)]
    targets += [head_dev(e) for e in range(1, NK)]
    targets += [weight_dev(e) for e in range(1, NK)]
    for t in targets:
        pl.semaphore_signal(barrier, inc=1, device_id=t, device_id_type=MESH)

    own_cols = pl.ds(pl.multiple_of(core * HD, HD), HD)
    other_cols = pl.ds(pl.multiple_of(other * HD, HD), HD)
    half_rows = (pl.multiple_of(core * HALF, HALF), pl.multiple_of(other * HALF, HALF))

    def rows_of(block, j):
        return pl.ds(pl.multiple_of(block * BLK + half_rows[j], HALF), HALF)

    own_rows = rows_of(1, 0)
    xq[own_rows, :] = q_in[:, own_cols]
    xk[own_rows, :] = k_in[:, own_cols]
    xv[own_rows, :] = v_in[:, own_cols]
    pl.semaphore_wait(barrier, len(targets))

    counter = [0]
    pending = []

    def remote(src, dst, target):
        n = counter[0]
        counter[0] += 1
        copy = pltpu.make_async_remote_copy(
            src_ref=src, dst_ref=dst, send_sem=send_sem.at[n], recv_sem=recv_sem.at[n],
            device_id=target, device_id_type=MESH,
        )
        copy.start()
        pending.append(copy)
        return copy

    def ring_send(arr, block_from, block_to, j, e):
        return remote(
            arr.at[rows_of(block_from, j), :], arr.at[rows_of(block_to, j), :], seq_dev(z_peer(e))
        )

    ring = {}

    def ring_start(name, arr, j):
        ring[name, 1, j] = ring_send(arr, 1, 2, j, 1)
        ring[name, 7, j] = ring_send(arr, 1, 8, j, NZ - 1)

    def ring_service(named, t):
        for name, arr in named:
            for j in (0, 1):
                for sign in (1, -1):
                    d = t if sign == 1 else NZ - t
                    ring[name, d, j].wait_recv()
                    if t < 3 or (t == 3 and (j == 0) == (sign == 1)):
                        e = 1 if sign == 1 else NZ - 1
                        ring[name, d + sign, j] = ring_send(arr, 1 + d, 1 + d + sign, j, e)

    def ring_last(named):
        for name, arr in named:
            for j in (0, 1):
                ring[name, 4, j].wait_recv()

    def to_sibling(src, arr):
        return remote(src.at[:, other_cols], arr.at[rows_of(1, 0), :], seq_dev(sibling))

    def to_pair(src, arr):
        return (
            remote(src.at[:, own_cols], arr.at[rows_of(0, 0), :], seq_dev(partner)),
            remote(src.at[:, other_cols], arr.at[rows_of(0, 0), :], seq_dev(diagonal)),
        )

    kv = (("k", xk), ("v", xv))
    qg = (("q", xq), ("g", xg))

    sib_k = to_sibling(k_in, xk)
    ring_start("k", xk, 0)
    sib_v = to_sibling(v_in, xv)
    ring_start("v", xv, 0)
    sib_q = to_sibling(q_in, xq)
    pair_q = to_pair(q_in, xq)
    sib_k.wait_recv()
    ring_start("k", xk, 1)
    sib_v.wait_recv()
    ring_start("v", xv, 1)

    ends = []
    total = jnp.int32(0)
    for j in range(DOCS):
        total = total + lengths[j]
        ends.append(total)

    def chip_group(zz, xx):
        return zz * 8 + xx * 4

    lane = lax.broadcasted_iota(jnp.int32, (GROUP, GROUP), 1)
    sub = lax.broadcasted_iota(jnp.int32, (GROUP, GROUP), 0)

    def place_body(g, _):
        xx = jnp.where(g < 4, 1 - x, x)
        pos = order[chip_group(z, xx) + g % 4] * GROUP + sub
        low = jnp.zeros((GROUP, GROUP), jnp.int32)
        high = jnp.full((GROUP, GROUP), 1 << 29, jnp.int32)
        for e in ends:
            low = jnp.maximum(low, jnp.where(pos >= e, e, 0))
            high = jnp.minimum(high, jnp.where(pos < e, e, 1 << 29))
        rows = pl.ds(pl.multiple_of(g * GROUP, GROUP), GROUP)
        first[rows, :] = low - lane
        place[rows, :] = pos - lane
        last[rows, :] = high - 1 - lane
        return 0

    lax.fori_loop(0, 8, place_body, 0)

    def base(d, j):
        return order[chip_group((z + NZ - d) % NZ, x) + j] * GROUP

    m_acc[...] = jnp.full((PAIR, HD), LOWEST, F32)
    l_acc[...] = jnp.zeros((PAIR, HD), F32)
    o_acc[...] = jnp.zeros((PAIR, HD), F32)
    dq_acc[...] = jnp.zeros((PAIR, HD), F32)
    dk_acc[...] = jnp.zeros((PAIR, HD), F32)
    dv_acc[...] = jnp.zeros((PAIR, HD), F32)

    def block_rows(d, n=1):
        return pl.ds((1 + d) * BLK, n * BLK)

    load_w.wait()
    load_g.wait()
    da_acc[...] = jnp.zeros((HALF, HALF), F32)

    def da_body(i, _):
        cols = pl.ds(pl.multiple_of(i * 1024, 1024), 1024)
        da_acc[...] += dot_nt(og[:, cols], wfull[:, cols])
        return 0

    lax.fori_loop(0, 4, da_body, 0)
    da[...] = da_acc[...].astype(BF16)
    xg[own_rows, :] = da[:, own_cols]
    sib_g = to_sibling(da, xg)

    col_half = pl.ds(pl.multiple_of(core * 256, 256), 256)
    w_copies = []
    for e in range(1, NK):
        kk = (k + e) % NK
        src = wfull.at[:, pl.ds(pl.multiple_of(kk * 512 + core * 256, 256), 256)]
        w_copies.append(remote(src, wg.at[k, :, col_half], weight_dev(e)))
    wg[k, :, :] = wfull[:, pl.ds(pl.multiple_of(k * 512, 512), 512)]

    pair_k = to_pair(k_in, xk)
    pair_v = to_pair(v_in, xv)

    def forward(blocks):
        def body(i, _):
            rows = pl.ds(pl.multiple_of(i * TILE, TILE), TILE)
            q = xq[rows, :]
            low, high = first[rows, :], place[rows, :]
            parts = []
            for d in blocks:
                logits = dot_nt(q, xk[block_rows(d), :])
                for j in range(4):
                    b = base(d, j)
                    part = logits[:, j * GROUP:(j + 1) * GROUP] * SCALE
                    parts.append(jnp.where((low <= b) & (high >= b), part, HIDDEN))
            top = functools.reduce(jnp.maximum, parts)
            old = m_acc[rows, :]
            new = jnp.maximum(old, jnp.max(top, axis=1, keepdims=True))
            factor = jnp.exp(old - new)
            weights = [jnp.exp(part - new) for part in parts]
            l_acc[rows, :] = l_acc[rows, :] * factor + functools.reduce(jnp.add, weights)
            m_acc[rows, :] = new
            product = o_acc[rows, :] * factor
            for n, d in enumerate(blocks):
                low_w = jnp.concatenate([w.astype(BF16) for w in weights[4 * n:4 * n + 4]], axis=1)
                product = product + dot_nn(low_w, xv[block_rows(d), :])
            o_acc[rows, :] = product
            return 0

        lax.fori_loop(0, PAIR // TILE, body, 0)

    sib_q.wait_recv()
    for c in pair_q:
        c.wait_recv()
    forward((0,))
    sib_g.wait_recv()
    pair_g = to_pair(da, xg)
    for t in (1, 2, 3):
        ring_service(kv, t)
        if t == 3:
            for j in (0, 1):
                ring_start("q", xq, j)
                ring_start("g", xg, j)
        forward((t, NZ - t))
    ring_last(kv)
    forward((4,))

    def close(rows):
        totals = jnp.maximum(jnp.sum(l_acc[rows, :], axis=1, keepdims=True), 1e-30)
        totals = jnp.broadcast_to(totals, (BLK, HD))
        return o_acc[rows, :] / totals, m_acc[rows, :] + jnp.log(totals)

    o_part, lse_part = close(pl.ds(0, BLK))
    o_send[...] = o_part.astype(BF16)
    st_send[0, :, :] = lse_part.T[0:8, :]
    copy_o = remote(o_send, o_recv, seq_dev(partner))
    copy_l = remote(st_send.at[0], st_recv, seq_dev(partner))
    ring_service(qg, 1)

    w_sib = []
    for e in range(1, NK):
        w_copies[e - 1].wait_recv()
        ref = wg.at[(k + NK - e) % NK, :, col_half]
        w_sib.append(remote(ref, ref, seq_dev(sibling)))

    o_own, lse_own = close(pl.ds(BLK, BLK))
    copy_l.wait_recv()
    copy_o.wait_recv()

    def to_col(row):
        return jnp.broadcast_to(row, (HD, BLK)).T

    lse_other = to_col(st_recv[0:1, :])
    top = jnp.maximum(lse_own, lse_other)
    lse = top + jnp.log(jnp.exp(lse_own - top) + jnp.exp(lse_other - top))
    merged = o_own * jnp.exp(lse_own - lse) + o_recv[...].astype(F32) * jnp.exp(lse_other - lse)
    attention = merged.astype(BF16)
    att[...] = attention
    delta = jnp.sum(
        attention.astype(F32) * xg[block_rows(0), :].astype(F32), axis=1, keepdims=True
    )
    delta = jnp.broadcast_to(delta, (BLK, HD))
    lse_col[BLK:, :] = lse
    delta_col[BLK:, :] = delta
    row8 = lax.broadcasted_iota(jnp.int32, (8, BLK), 0)
    stats = jnp.where(row8 == 0, lse.T[0:8, :], delta.T[0:8, :])
    st_z[0, :, :] = stats
    copy_sp = remote(st_z.at[0], st_par, seq_dev(partner))
    copy_sz = [remote(st_z.at[0], st_z.at[e], seq_dev(z_peer(e))) for e in range(1, NZ)]
    copy_a = remote(
        att.at[pl.ds(half_rows[1], HALF), :], attg.at[k, :, own_cols], seq_dev(sibling)
    )
    attg[k, :, own_cols] = att[pl.ds(half_rows[0], HALF), :]

    def query_side(u0, u1):
        def body(n, _):
            i, u = n % (PAIR // TILE), n // (PAIR // TILE)
            rows = pl.ds(pl.multiple_of(i * TILE, TILE), TILE)
            keys = pl.ds(pl.multiple_of(BLK + u * PAIR, BLK), PAIR)
            low, high = first[rows, :], place[rows, :]
            log_t, dlt = lse_col[rows, :], delta_col[rows, :]
            key = xk[keys, :]
            logits = dot_nt(xq[rows, :], key)
            dprobs = dot_nt(xg[rows, :], xv[keys, :])
            out = []
            for j in range(8):
                b = base(2 * u + j // 4, j % 4)
                cols = slice(j * GROUP, (j + 1) * GROUP)
                part = jnp.where(
                    (low <= b) & (high >= b), logits[:, cols] * SCALE - log_t, HIDDEN
                )
                out.append((jnp.exp(part) * (dprobs[:, cols] - dlt)).astype(BF16))
            dq_acc[rows, :] += dot_nn(jnp.concatenate(out, axis=1), key)
            return 0

        lax.fori_loop(u0 * (PAIR // TILE), u1 * (PAIR // TILE), body, 0)

    def key_side(blocks):
        def body(i, _):
            keys = pl.ds(pl.multiple_of(i * TILE, TILE), TILE)
            low, high = place[keys, :], last[keys, :]
            key, value = xk[keys, :], xv[keys, :]
            dk, dv = dk_acc[keys, :], dv_acc[keys, :]
            for d in blocks:
                query, grad = xq[block_rows(d), :], xg[block_rows(d), :]
                logits = dot_nt(key, query)
                dprobs = dot_nt(value, grad)
                probs, scores = [], []
                for j in range(4):
                    b = base(d, j)
                    cols = slice(j * GROUP, (j + 1) * GROUP)
                    log_t = st_z[d, 0:1, cols]
                    dlt = st_z[d, 1:2, cols]
                    part = jnp.where(
                        (low <= b) & (high >= b), logits[:, cols] * SCALE - log_t, HIDDEN
                    )
                    prob = jnp.exp(part)
                    probs.append(prob.astype(BF16))
                    scores.append((prob * (dprobs[:, cols] - dlt)).astype(BF16))
                dv = dv + dot_nn(jnp.concatenate(probs, axis=1), grad)
                dk = dk + dot_nn(jnp.concatenate(scores, axis=1), query)
            dk_acc[keys, :] = dk
            dv_acc[keys, :] = dv
            return 0

        lax.fori_loop(0, PAIR // TILE, body, 0)

    def send_grad(n, acc, scale):
        def piece(block, j):
            return (acc[rows_of(block, j), :] * scale).astype(BF16)

        copies = []
        for m, (block, j, t) in enumerate(((1, 1, sibling), (0, 0, partner), (0, 1, diagonal))):
            grad_send[n, m, :, :] = piece(block, j)
            copies.append(remote(grad_send.at[n, m], grad_recv.at[n, m], seq_dev(t)))
        return copies

    def finish_grad(n, acc, scale, copies, out):
        for c in copies:
            c.wait_recv()
        mine = acc[rows_of(1, 0), :] * scale + grad_recv[n, 1, :, :].astype(F32)
        theirs = grad_recv[n, 0, :, :].astype(F32) + grad_recv[n, 2, :, :].astype(F32)
        out[:, own_cols] = mine.astype(BF16)
        out[:, other_cols] = theirs.astype(BF16)

    ring_service(qg, 2)
    for c in pair_k + pair_v + pair_g:
        c.wait_recv()
    copy_a.wait_recv()
    att_copies = [remote(attg.at[k], attg.at[k], head_dev(e)) for e in range(1, NK)]
    key_side((0,))
    copy_sp.wait_recv()
    lse_col[:BLK, :] = to_col(st_par[0:1, :])
    delta_col[:BLK, :] = to_col(st_par[1:2, :])
    query_side(0, 2)
    ring_service(qg, 3)
    query_side(2, 4)
    grads_q = send_grad(0, dq_acc, SCALE)
    for c in copy_sz:
        c.wait_recv()
    key_side((1, 7))
    key_side((2, 6))

    for c in att_copies + w_sib:
        c.wait_recv()

    def project(i, total):
        return total + dot_nn(attg[i, :, :], wg[i, :, :])

    layer_out[...] = lax.fori_loop(0, NK, project, jnp.zeros((HALF, 512), F32)).astype(BF16)

    key_side((3, 5))
    ring_last(qg)
    key_side((4,))
    grads_k = send_grad(1, dk_acc, SCALE)
    grads_v = send_grad(2, dv_acc, 1.0)
    finish_grad(0, dq_acc, SCALE, grads_q, dq_out)
    finish_grad(1, dk_acc, SCALE, grads_k, dk_out)
    finish_grad(2, dv_acc, 1.0, grads_v, dv_out)
    for c in pending:
        c.wait_send()


COPIES = 128


def per_device(queries, key_vectors, value_vectors, group_order, doc_lengths, out_grad, out_weight):
    vmem = pl.BlockSpec(memory_space=pltpu.VMEM)
    smem = pl.BlockSpec(memory_space=pltpu.SMEM)
    hbm = pl.BlockSpec(memory_space=pl.ANY)
    blocks = pltpu.VMEM((9 * BLK, HD), BF16)
    pair_f32 = pltpu.VMEM((PAIR, HD), F32)
    pair_int = pltpu.VMEM((PAIR, HD), jnp.int32)
    return pl.pallas_call(
        kernel,
        out_shape=(
            jax.ShapeDtypeStruct((HALF, 512), BF16),
            jax.ShapeDtypeStruct((HALF, 2 * HD), BF16),
            jax.ShapeDtypeStruct((HALF, 2 * HD), BF16),
            jax.ShapeDtypeStruct((HALF, 2 * HD), BF16),
        ),
        in_specs=[smem, smem, vmem, vmem, vmem, hbm, hbm],
        out_specs=(vmem, vmem, vmem, vmem),
        scratch_shapes=[
            blocks, blocks, blocks, blocks,
            pltpu.VMEM((HALF, 4096), BF16),
            pltpu.VMEM((HALF, 4096), BF16),
            pltpu.VMEM((NK, HALF, 512), BF16),
            pltpu.VMEM((HALF, HALF), BF16),
            pltpu.VMEM((HALF, HALF), F32),
            pltpu.VMEM((BLK, HD), BF16),
            pltpu.VMEM((NK, HALF, HALF), BF16),
            pair_int, pair_int, pair_int,
            pair_f32, pair_f32, pair_f32, pair_f32, pair_f32, pair_f32, pair_f32, pair_f32,
            pltpu.VMEM((BLK, HD), BF16),
            pltpu.VMEM((BLK, HD), BF16),
            pltpu.VMEM((1, 8, BLK), F32),
            pltpu.VMEM((8, BLK), F32),
            pltpu.VMEM((NZ, 8, BLK), F32),
            pltpu.VMEM((8, BLK), F32),
            pltpu.VMEM((3, 3, HALF, HD), BF16),
            pltpu.VMEM((3, 3, HALF, HD), BF16),
            pltpu.SemaphoreType.DMA((COPIES,)),
            pltpu.SemaphoreType.DMA((COPIES,)),
            pltpu.SemaphoreType.DMA((2,)),
        ],
        compiler_params=pltpu.CompilerParams(
            collective_id=0, has_side_effects=True, vmem_limit_bytes=48 * 1024 * 1024
        ),
        name="attention_grads",
    )(group_order, doc_lengths, queries, key_vectors, value_vectors, out_grad, out_weight)


def solution(mesh):
    return jax.shard_map(
        per_device,
        mesh=mesh,
        in_specs=(
            P("seq", "head"),
            P("seq", "head"),
            P("seq", "head"),
            P(),
            P(),
            P("seq", None),
            P("head", None),
        ),
        out_specs=(P("seq", "head"), P("seq", "head"), P("seq", "head"), P("seq", "head")),
        check_vma=False,
    )
```

time: 767 us -> 97 us (0.13)
  matrix products: 276 us -> 0 us
  starting transfers between devices: 191 us -> 0 us
  waiting for transfers between devices: 126 us -> 0 us
  other arithmetic: 86.4 us -> 0 us
  Pallas kernels: 0 us -> 86.2 us
  local copies, waits for them, and re-layouts: 64.5 us -> 9.86 us
  between operations: 14 us -> 0.66 us
    dot_general x164 -> x0, matrix products: 276 us -> none  [the longest x32 60.8 us: tile_grads(): jnp.einsum('hqk,qhd->khd', dscores, query_block, preferred_element_type=j...]
    ppermute x156 -> x0, starting transfers between devices: 190 us -> none  [from_behind(): return lax.ppermute(block, axis, route)]
    all_gather x2 -> x0, waiting for transfers between devices: 115 us -> none  [the longest x1 60.1 us: per_device(): lax.all_gather(key_vectors, 'seq', axis=0, tiled=True)]
    pallas_call x0 -> x1, Pallas kernels: none -> 86.2 us  [per_device(): pl.pallas_call(kernel, out_shape=(jax.ShapeDtypeStruct((HALF, 512), BF16)...]
    reduce_sum x67 -> x0, other arithmetic: 54.1 us -> none  [the longest x33 25 us: group_lookup(): chosen = jnp.sum(jnp.where(slot_match, group_order[None, :], 0), axis=1)]
    while x126 -> x0, local copies, waits for them, and re-layouts: 47.4 us -> none
    and x33 -> x0, other arithmetic: 28.3 us -> none  [visible_pairs(): (key_pos[None, :] <= query_pos[:, None]) & (key_doc[None, :] == query_doc...]
    ppermute x156 -> x0, waiting for transfers between devices: 10.5 us -> none  [from_behind(): return lax.ppermute(block, axis, route)]
  transfers between devices with their start and end apart: 159 -> 0, of which waited for: 6 -> 0; matrix products, arithmetic and copies ran while one was open for 53% -> 0% of each run, Pallas kernels for 0% -> 0%
where the time goes in v1:
time: 97 us; the launch traced here: 96.7 us
  Pallas kernels  86.2 us (89%)
  local copies, waits for them, and re-layouts  9.86 us (10%)
    pallas_call x1, Pallas kernels, per_device(): pl.pallas_call(kernel, out_shape=(jax.ShapeDtypeStruct((HALF, 512), BF16)...  86.2 us
    unnamed x18, local copies, waits for them, and re-layouts  9.86 us

profile of v1, /device:TPU:1, one launch (start us, length us, event | category | flops | bytes accessed | tf_op | source)
XLA Modules:
  0.0 96.7 jit_solution(797375217027835531)
XLA Ops:
  0.6 0.0 copy-start
  0.6 1.6 %copy-done = bf16[256,4096]{1,0:T(8,128)(2,1)S(1)} copy-done((bf16[256,4096]{1,0:T(8,128)(2,1)S(1)}, bf16[256,4096]{1,0:T(8,128)(2,1)}, u32[]{:S(2)}) %copy-start) | copy-done | bytes 2097176
  2.2 0.0 copy-start.1
  2.2 1.6 %copy-done.1 = bf16[256,4096]{1,0:T(8,128)(2,1)S(1)} copy-done((bf16[256,4096]{1,0:T(8,128)(2,1)S(1)}, bf16[256,4096]{1,0:T(8,128)(2,1)}, u32[]{:S(2)}) %copy-start.1) | copy-done | bytes 2097176
  3.8 0.0 copy-start.2
  3.8 0.9 copy-done.2
  4.7 0.0 copy-start.3
  4.7 0.9 copy-done.3
  5.6 0.0 copy-start.4
  5.6 0.9 copy-done.4
  6.5 0.0 copy-start.5
  6.5 0.7 copy-done.5
  7.2 0.0 copy-start.6
  7.2 0.7 copy-done.6
  7.8 86.2 %attention_grads.1 = (bf16[256,512]{1,0:T(8,128)(2,1)S(1)}, bf16[256,256]{1,0:T(8,128)(2,1)S(1)}, bf16[256,256]{1,0:T(8,128)(2,1)S(1)}, bf16[256,256]{1,0:T(8,128)(2,1)S(1)}) custom-call(s32[64]{0:T(128)S(1)} %copy-done.5, s32[8]{0:T(128)S(1)} %copy-done.6, bf16[256,256]{1,0:T(8,128)(2,1)S(1)} %copy-done.2, bf16[256,256]{1,0:T(8,128)(2,1)S(1)} %copy-done.3, ...), custom_call_target="tpu_custom_call" | custom-call | tf_op jit(solution)/shard_map/attention_grads/pallas_call | solution.py:435
  94.1 0.7 copy.15
  94.8 0.7 copy.16
  95.4 0.7 copy.17
  96.1 0.7 copy.18
Async XLA Ops:
  0.6 1.6 %copy-start = (bf16[256,4096]{1,0:T(8,128)(2,1)S(1)}, bf16[256,4096]{1,0:T(8,128)(2,1)}, u32[]{:S(2)}) copy-start(bf16[256,4096]{1,0:T(8,128)(2,1)} %og_hbm.1) | copy-start | bytes 6291460
  2.2 1.6 %copy-start.1 = (bf16[256,4096]{1,0:T(8,128)(2,1)S(1)}, bf16[256,4096]{1,0:T(8,128)(2,1)}, u32[]{:S(2)}) copy-start(bf16[256,4096]{1,0:T(8,128)(2,1)} %w_hbm.1) | copy-start | bytes 6291460
  3.8 0.9 copy-start.2
  4.7 0.9 copy-start.3
  5.6 0.9 copy-start.4
  6.5 0.7 copy-start.5
  7.2 0.7 copy-start.6

commit v2 on v1

v2 whole, which is shorter than its diff:
```python
import functools
import math

import jax
import jax.numpy as jnp
from jax import lax
from jax.experimental import pallas as pl
from jax.experimental.pallas import tpu as pltpu
from jax.sharding import PartitionSpec as P

HD = 128
GROUP = 128
DOCS = 8
NZ = 8
NK = 8
BLK = 512
HALF = 256
PAIR = 2 * BLK
KEYS, VALUES, QUERIES, GRADS = range(4)
LOG2E = math.log2(math.e)
SCALE = 1.0 / math.sqrt(HD)
SCALE2 = SCALE * LOG2E
HIDDEN = -1e30
LOWEST = -5e29
F32 = jnp.float32
BF16 = jnp.bfloat16
MESH = pl.DeviceIdType.MESH


def dot_nt(a, b):
    return lax.dot_general(a, b, (((1,), (1,)), ((), ())), preferred_element_type=F32)


def dot_nn(a, b):
    return jnp.dot(a, b, preferred_element_type=F32)


def kernel(
    order_hbm, lengths_hbm, q_hbm, k_hbm, v_hbm, og_hbm, w_hbm,
    layer_hbm, dq_hbm, dk_hbm, dv_hbm,
    order, lengths, q_in, k_in, v_in, layer_out, grad_out,
    xa,
    og, wfull, wg, da, da_acc, att, attg,
    first, place, last,
    o_acc, m_acc, l_acc, a1_acc, a2_acc, dq_acc, dk_acc, dv_acc,
    o_send, o_recv, st_send, st_recv, st_z, st_par, grad_send, grad_recv,
    send_sem, recv_sem, ring_send_sem, ring_recv_sem, stat_send_sem, stat_recv_sem, local_sem,
):
    s = lax.axis_index("seq")
    k = lax.axis_index("head")
    core = s % 2
    other = 1 - core
    x = (s // 2) % 2
    z = s // 4
    sibling = s + 1 - 2 * core
    partner = s + 2 - 4 * x
    diagonal = partner + 1 - 2 * core

    def z_peer(e):
        return ((z + e) % NZ) * 4 + s % 4

    def seq_dev(t):
        return (t, k)

    def head_dev(e):
        return (s, (k + e) % NK)

    def weight_dev(e):
        kk = (k + e) % NK
        diff = (kk // 4 - k // 4) * (kk // 4 - k // 4)
        return (s + diff * (2 - 4 * x), kk)

    barrier = pltpu.get_barrier_semaphore()
    targets = [seq_dev(sibling), seq_dev(partner), seq_dev(diagonal)]
    targets += [seq_dev(z_peer(e)) for e in range(1, NZ)]
    targets += [head_dev(e) for e in range(1, NK)]
    targets += [weight_dev(e) for e in range(1, NK)]
    for t in targets:
        pl.semaphore_signal(barrier, inc=1, device_id=t, device_id_type=MESH)

    def local(src, dst, n):
        copy = pltpu.make_async_copy(src, dst, local_sem.at[n])
        copy.start()
        return copy

    loads = [
        local(src, dst, n)
        for n, (src, dst) in enumerate((
            (order_hbm, order), (lengths_hbm, lengths),
            (k_hbm, k_in), (v_hbm, v_in), (q_hbm, q_in), (w_hbm, wfull), (og_hbm, og),
        ))
    ]

    own_cols = pl.ds(pl.multiple_of(core * HD, HD), HD)
    other_cols = pl.ds(pl.multiple_of(other * HD, HD), HD)
    xk, xv, xq, xg = (xa.at[a] for a in (KEYS, VALUES, QUERIES, GRADS))
    half_rows = (pl.multiple_of(core * HALF, HALF), pl.multiple_of(other * HALF, HALF))

    def rows_of(block, j):
        return pl.ds(pl.multiple_of(block * BLK + half_rows[j], HALF), HALF)

    for c in loads[:2]:
        c.wait()
    ends = []
    total = jnp.int32(0)
    for j in range(DOCS):
        total = total + lengths[j]
        ends.append(total)

    def chip_group(zz, xx):
        return zz * 8 + xx * 4

    lane = lax.broadcasted_iota(jnp.int32, (GROUP, GROUP), 1)
    sub = lax.broadcasted_iota(jnp.int32, (GROUP, GROUP), 0)

    def place_body(g, _):
        xx = jnp.where(g < 4, 1 - x, x)
        pos = order[chip_group(z, xx) + g % 4] * GROUP + sub
        low = jnp.zeros((GROUP, GROUP), jnp.int32)
        high = jnp.full((GROUP, GROUP), 1 << 29, jnp.int32)
        for e in ends:
            low = jnp.maximum(low, jnp.where(pos >= e, e, 0))
            high = jnp.minimum(high, jnp.where(pos < e, e, 1 << 29))
        rows = pl.ds(pl.multiple_of(g * GROUP, GROUP), GROUP)
        first[rows, :] = low - lane
        place[rows, :] = pos - lane
        last[rows, :] = high - 1 - lane
        return 0

    lax.fori_loop(0, 8, place_body, 0)

    def base(d, j):
        return order[chip_group((z + NZ - d) % NZ, x) + j] * GROUP

    own_rows = rows_of(1, 0)
    for c in loads[2:5]:
        c.wait()
    xk[own_rows, :] = k_in[:, own_cols]
    xv[own_rows, :] = v_in[:, own_cols]
    xq[own_rows, :] = q_in[:, own_cols]
    m_acc[...] = jnp.full((PAIR, HD), LOWEST, F32)
    for acc in (l_acc, o_acc, a1_acc, a2_acc, dk_acc, dv_acc):
        acc[...] = jnp.zeros((PAIR, HD), F32)

    for c in loads[5:]:
        c.wait()
    da_acc[...] = jnp.zeros((HALF, HALF), F32)

    def da_body(i, _):
        cols = pl.ds(pl.multiple_of(i * 1024, 1024), 1024)
        da_acc[...] += dot_nt(og[:, cols], wfull[:, cols])
        return 0

    lax.fori_loop(0, 4, da_body, 0)
    da[...] = da_acc[...].astype(BF16)
    xg[own_rows, :] = da[:, own_cols]

    pl.semaphore_wait(barrier, len(targets))

    counter = [0]
    pending = []

    def plan(src, dst, target):
        n = counter[0]
        counter[0] += 1
        copy = pltpu.make_async_remote_copy(
            src_ref=src, dst_ref=dst, send_sem=send_sem.at[n], recv_sem=recv_sem.at[n],
            device_id=target, device_id_type=MESH,
        )
        pending.append(copy)
        return copy

    def remote(src, dst, target):
        copy = plan(src, dst, target)
        copy.start()
        return copy

    def ring_copy(a, back, t, j):
        src, dst = (1 + (9 - t) % NZ, 9 - t) if back else (t, 1 + t)
        return pltpu.make_async_remote_copy(
            src_ref=xa.at[a, rows_of(src, j), :], dst_ref=xa.at[a, rows_of(dst, j), :],
            send_sem=ring_send_sem.at[a, back, t - 1, j],
            recv_sem=ring_recv_sem.at[a, back, t - 1, j],
            device_id=seq_dev(z_peer(NZ - 1 if back else 1)), device_id_type=MESH,
        )

    def ring_start(a, j):
        for back in (0, 1):
            ring_copy(a, back, 1, j).start()

    def ring_service(a, t):
        for j in (0, 1):
            for back in (0, 1):
                if j == back:
                    ring_copy(a, back, t, j).wait_recv()

                    @pl.when(t < 4)
                    def _():
                        ring_copy(a, back, t + 1, j).start()
                else:
                    @pl.when(t < 4)
                    def _():
                        ring_copy(a, back, t, j).wait_recv()

                    @pl.when(t < 3)
                    def _():
                        ring_copy(a, back, t + 1, j).start()

    def to_sibling(src, arr):
        return remote(src.at[:, other_cols], arr.at[rows_of(1, 0), :], seq_dev(sibling))

    def to_pair(src, arr):
        return (
            remote(src.at[:, own_cols], arr.at[rows_of(0, 0), :], seq_dev(partner)),
            remote(src.at[:, other_cols], arr.at[rows_of(0, 0), :], seq_dev(diagonal)),
        )

    sib_k = to_sibling(k_in, xk)
    sib_v = to_sibling(v_in, xv)
    ring_start(KEYS, 0)
    ring_start(VALUES, 0)
    sib_q = to_sibling(q_in, xq)
    sib_g = to_sibling(da, xg)
    pair_q = to_pair(q_in, xq)
    pair_g = to_pair(da, xg)
    sib_k.wait_recv()
    ring_start(KEYS, 1)
    sib_v.wait_recv()
    ring_start(VALUES, 1)
    pair_k = to_pair(k_in, xk)
    pair_v = to_pair(v_in, xv)

    col_half = pl.ds(pl.multiple_of(core * 256, 256), 256)
    w_copies = []
    for e in range(1, NK):
        kk = (k + e) % NK
        src = wfull.at[:, pl.ds(pl.multiple_of(kk * 512 + core * 256, 256), 256)]
        w_copies.append(remote(src, wg.at[k, :, col_half], weight_dev(e)))
    wg[k, :, :] = wfull[:, pl.ds(pl.multiple_of(k * 512, 512), 512)]
    w_sib = []
    for e in range(1, NK):
        ref = wg.at[(k + NK - e) % NK, :, col_half]
        w_sib.append(plan(ref, ref, seq_dev(sibling)))

    copy_l = plan(st_send.at[0], st_recv, seq_dev(partner))
    copy_o = plan(o_send, o_recv, seq_dev(partner))
    att_copies = [plan(attg.at[k], attg.at[k], head_dev(e)) for e in range(1, NK)]
    grads = [
        [
            plan(grad_send.at[n, m], grad_recv.at[n, m], seq_dev(t))
            for m, t in enumerate((sibling, partner, diagonal))
        ]
        for n in range(3)
    ]

    def block_rows(d):
        return pl.ds(pl.multiple_of((1 + d) * BLK, BLK), BLK)

    def pair_of(p):
        return ((NZ - p) % NZ, p + 1)

    own, theirs = pl.ds(BLK, BLK), pl.ds(0, BLK)

    def forward(blocks, rows):
        q, grad = xq[rows, :], xg[rows, :]
        low, high = first[rows, :], place[rows, :]
        parts, dprobs = [], []
        for d in blocks:
            logits = dot_nt(q, xk[block_rows(d), :])
            dprobs.append(dot_nt(grad, xv[block_rows(d), :]))
            for j in range(4):
                b = base(d, j)
                part = logits[:, j * GROUP:(j + 1) * GROUP] * SCALE2
                parts.append(jnp.where((low <= b) & (high >= b), part, HIDDEN))
        top = functools.reduce(jnp.maximum, parts)
        old = m_acc[rows, :]
        new = jnp.maximum(old, jnp.max(top, axis=1, keepdims=True))
        factor = jnp.exp2(old - new)
        weights = [jnp.exp2(part - new) for part in parts]
        l_acc[rows, :] = l_acc[rows, :] * factor + functools.reduce(jnp.add, weights)
        m_acc[rows, :] = new
        o_sum = o_acc[rows, :] * factor
        a1_sum = a1_acc[rows, :] * factor
        a2_sum = a2_acc[rows, :] * factor
        for n, d in enumerate(blocks):
            key = xk[block_rows(d), :]
            mine = weights[4 * n:4 * n + 4]
            both = dot_nn(
                jnp.concatenate([w.astype(BF16) for w in mine], axis=1),
                jnp.concatenate([xv[block_rows(d), :], key], axis=1),
            )
            o_sum = o_sum + both[:, :HD]
            a2_sum = a2_sum + both[:, HD:]
            scores = [
                (w * dprobs[n][:, j * GROUP:(j + 1) * GROUP]).astype(BF16)
                for j, w in enumerate(mine)
            ]
            a1_sum = a1_sum + dot_nn(jnp.concatenate(scores, axis=1), key)
        o_acc[rows, :] = o_sum
        a1_acc[rows, :] = a1_sum
        a2_acc[rows, :] = a2_sum

    def close(rows):
        totals = jnp.maximum(jnp.sum(l_acc[rows, :], axis=1, keepdims=True), 1e-30)
        totals = jnp.broadcast_to(totals, (BLK, HD))
        return o_acc[rows, :] / totals, m_acc[rows, :] + jnp.log(totals) * LOG2E

    for c in (sib_q, sib_g) + pair_q + pair_g:
        c.wait_recv()
    ring_service(KEYS, 1)

    def forward_step(n, _):
        p = n // 2

        @pl.when(n < 7)
        def _():
            ring_service(1 - n % 2, (n + 1) // 2 + 1)

        @pl.when(n == 4)
        def _():
            for a in (QUERIES, GRADS):
                for j in (0, 1):
                    ring_start(a, j)

        @pl.when(n == 7)
        def _():
            o_part, lse_part = close(theirs)
            o_send[...] = o_part.astype(BF16)
            st_send[0, :, :] = lse_part.T[0:8, :]
            copy_l.start()
            copy_o.start()

        forward(pair_of(p), pl.ds(pl.multiple_of((n % 2) * BLK, BLK), BLK))
        return 0

    lax.fori_loop(0, 8, forward_step, 0)
    ring_service(QUERIES, 1)
    o_own, lse_own = close(own)
    ring_service(GRADS, 1)
    copy_l.wait_recv()
    copy_o.wait_recv()

    def to_col(row):
        return jnp.broadcast_to(row, (HD, BLK)).T

    lse_other = to_col(st_recv[0:1, :])
    top = jnp.maximum(lse_own, lse_other)
    lse = top + jnp.log(jnp.exp2(lse_own - top) + jnp.exp2(lse_other - top)) * LOG2E
    merged = o_own * jnp.exp2(lse_own - lse) + o_recv[...].astype(F32) * jnp.exp2(lse_other - lse)
    attention = merged.astype(BF16)
    att[...] = attention
    delta = jnp.sum(
        attention.astype(F32) * xg[block_rows(0), :].astype(F32), axis=1, keepdims=True
    )
    delta = jnp.broadcast_to(delta, (BLK, HD))
    row8 = lax.broadcasted_iota(jnp.int32, (8, BLK), 0)
    st_z[0, :, :] = jnp.where(row8 == 0, lse.T[0:8, :], delta.T[0:8, :])
    def stats_copy(e):
        return pltpu.make_async_remote_copy(
            src_ref=st_z.at[0], dst_ref=st_z.at[e],
            send_sem=stat_send_sem.at[e], recv_sem=stat_recv_sem.at[e],
            device_id=seq_dev(z_peer(e)), device_id_type=MESH,
        )

    for e in (1, 7, 2, 6, 3, 5, 4):
        stats_copy(e).start()
    copy_sp = remote(st_z.at[0], st_par, seq_dev(partner))
    copy_a = remote(
        att.at[pl.ds(half_rows[1], HALF), :], attg.at[k, :, own_cols], seq_dev(sibling)
    )
    attg[k, :, own_cols] = att[pl.ds(half_rows[0], HALF), :]

    def close_queries(rows, lse_rows, delta_rows):
        factor = jnp.exp2(m_acc[rows, :] - lse_rows) * SCALE
        dq_acc[rows, :] = (a1_acc[rows, :] - delta_rows * a2_acc[rows, :]) * factor

    def key_side(blocks, keys):
        low, high = place[keys, :], last[keys, :]
        key, value = xk[keys, :], xv[keys, :]
        dk, dv = dk_acc[keys, :], dv_acc[keys, :]
        for d in blocks:
            query, grad = xq[block_rows(d), :], xg[block_rows(d), :]
            logits = dot_nt(key, query)
            dprobs = dot_nt(value, grad)
            probs, scores = [], []
            for j in range(4):
                b = base(d, j)
                cols = slice(j * GROUP, (j + 1) * GROUP)
                log_t = st_z[d, 0:1, cols]
                dlt = st_z[d, 1:2, cols]
                part = jnp.where(
                    (low <= b) & (high >= b), logits[:, cols] * SCALE2 - log_t, HIDDEN
                )
                prob = jnp.exp2(part)
                probs.append(prob.astype(BF16))
                scores.append((prob * (dprobs[:, cols] - dlt)).astype(BF16))
            dv = dv + dot_nn(jnp.concatenate(probs, axis=1), grad)
            dk = dk + dot_nn(jnp.concatenate(scores, axis=1), query)
        dk_acc[keys, :] = dk
        dv_acc[keys, :] = dv

    def send_grad(n, acc, scale, m):
        block, j = ((1, 1), (0, 0), (0, 1))[m]
        grad_send[n, m, :, :] = (acc[rows_of(block, j), :] * scale).astype(BF16)
        grads[n][m].start()

    def finish_grad(n, acc, scale, out):
        for c in grads[n]:
            c.wait_recv()
        mine = acc[rows_of(1, 0), :] * scale + grad_recv[n, 1, :, :].astype(F32)
        not_mine = grad_recv[n, 0, :, :].astype(F32) + grad_recv[n, 2, :, :].astype(F32)
        grad_out[n, :, own_cols] = mine.astype(BF16)
        grad_out[n, :, other_cols] = not_mine.astype(BF16)
        return local(grad_out.at[n], out, 7 + n)

    close_queries(own, lse, delta)
    for c in pair_k + pair_v:
        c.wait_recv()

    def key_step(n, _):
        p = n // 2

        @pl.when(n > 0)
        def _():
            @pl.when(n < 7)
            def _():
                ring_service(3 - n % 2, (n + 1) // 2 + 1)

        @pl.when(n % 2 == 0)
        def _():
            stats_copy(p + 1).wait_recv()

            @pl.when(p > 0)
            def _():
                stats_copy(NZ - p).wait_recv()

        @pl.when(n == 1)
        def _():
            copy_a.wait_recv()
            for c in att_copies:
                c.start()
            copy_sp.wait_recv()
            close_queries(theirs, to_col(st_par[0:1, :]), to_col(st_par[1:2, :]))
            for m in (1, 2, 0):
                send_grad(0, dq_acc, 1.0, m)

        @pl.when(n == 2)
        def _():
            for c, d in zip(w_copies, w_sib):
                c.wait_recv()
                d.start()

        @pl.when(n == 7)
        def _():
            for m in (1, 2):
                send_grad(2, dv_acc, 1.0, m)
                send_grad(1, dk_acc, SCALE, m)

        key_side(pair_of(p), pl.ds(pl.multiple_of((n % 2) * BLK, BLK), BLK))
        return 0

    lax.fori_loop(0, 8, key_step, 0)
    send_grad(2, dv_acc, 1.0, 0)
    send_grad(1, dk_acc, SCALE, 0)
    stores = [finish_grad(0, dq_acc, 1.0, dq_hbm)]

    for c in att_copies + w_sib:
        c.wait_recv()

    def project(i, total):
        return total + dot_nn(attg[i, :, :], wg[i, :, :])

    layer_out[...] = lax.fori_loop(0, NK, project, jnp.zeros((HALF, 512), F32)).astype(BF16)
    stores.append(local(layer_out, layer_hbm, 10))
    stores.append(finish_grad(2, dv_acc, 1.0, dv_hbm))
    stores.append(finish_grad(1, dk_acc, SCALE, dk_hbm))
    for c in stores:
        c.wait()
    for c in pending:
        c.wait_send()
    for e in range(1, NZ):
        stats_copy(e).wait_send()

    def drain(a, _):
        for j in (0, 1):
            for back in (0, 1):
                for t in range(1, 5 if j == back else 4):
                    ring_copy(a, back, t, j).wait_send()
        return 0

    lax.fori_loop(0, 4, drain, 0)


COPIES = 56
VMEM_BYTES = 62 * 1024 * 1024


def emit(a, b, c, d, a_out, b_out, c_out, d_out, a_buf, b_buf, c_buf, d_buf, sem):
    steps = ((a, a_buf, a_out), (b, b_buf, b_out), (c, c_buf, c_out), (d, d_buf, d_out))
    loads = [pltpu.make_async_copy(t[0], t[1], sem.at[0, n]) for n, t in enumerate(steps)]
    stores = [pltpu.make_async_copy(t[1], t[2], sem.at[1, n]) for n, t in enumerate(steps)]
    for copy in loads:
        copy.start()
    for load, store in zip(loads, stores):
        load.wait()
        store.start()
    for copy in stores:
        copy.wait()


def per_device(queries, key_vectors, value_vectors, group_order, doc_lengths, out_grad, out_weight):
    hbm = pl.BlockSpec(memory_space=pl.ANY)
    local = pltpu.VMEM((HALF, 2 * HD), BF16)
    pair_f32 = pltpu.VMEM((PAIR, HD), F32)
    pair_int = pltpu.VMEM((PAIR, HD), jnp.int32)
    results = pl.pallas_call(
        kernel,
        out_shape=(
            jax.ShapeDtypeStruct((HALF, 512), BF16),
            jax.ShapeDtypeStruct((HALF, 2 * HD), BF16),
            jax.ShapeDtypeStruct((HALF, 2 * HD), BF16),
            jax.ShapeDtypeStruct((HALF, 2 * HD), BF16),
        ),
        in_specs=[hbm] * 7,
        out_specs=(hbm, hbm, hbm, hbm),
        scratch_shapes=[
            pltpu.SMEM((64,), jnp.int32),
            pltpu.SMEM((DOCS,), jnp.int32),
            local, local, local,
            pltpu.VMEM((HALF, 512), BF16),
            pltpu.VMEM((3, HALF, 2 * HD), BF16),
            pltpu.VMEM((4, 9 * BLK, HD), BF16),
            pltpu.VMEM((HALF, 4096), BF16),
            pltpu.VMEM((HALF, 4096), BF16),
            pltpu.VMEM((NK, HALF, 512), BF16),
            pltpu.VMEM((HALF, HALF), BF16),
            pltpu.VMEM((HALF, HALF), F32),
            pltpu.VMEM((BLK, HD), BF16),
            pltpu.VMEM((NK, HALF, HALF), BF16),
            pair_int, pair_int, pair_int,
            pair_f32, pair_f32, pair_f32, pair_f32, pair_f32, pair_f32, pair_f32, pair_f32,
            pltpu.VMEM((BLK, HD), BF16),
            pltpu.VMEM((BLK, HD), BF16),
            pltpu.VMEM((1, 8, BLK), F32),
            pltpu.VMEM((8, BLK), F32),
            pltpu.VMEM((NZ, 8, BLK), F32),
            pltpu.VMEM((8, BLK), F32),
            pltpu.VMEM((3, 3, HALF, HD), BF16),
            pltpu.VMEM((3, 3, HALF, HD), BF16),
            pltpu.SemaphoreType.DMA((COPIES,)),
            pltpu.SemaphoreType.DMA((COPIES,)),
            pltpu.SemaphoreType.DMA((4, 2, 4, 2)),
            pltpu.SemaphoreType.DMA((4, 2, 4, 2)),
            pltpu.SemaphoreType.DMA((NZ,)),
            pltpu.SemaphoreType.DMA((NZ,)),
            pltpu.SemaphoreType.DMA((11,)),
        ],
        compiler_params=pltpu.CompilerParams(
            collective_id=0, has_side_effects=True, vmem_limit_bytes=VMEM_BYTES
        ),
        name="attention_grads",
    )(group_order, doc_lengths, queries, key_vectors, value_vectors, out_grad, out_weight)
    return pl.pallas_call(
        emit,
        out_shape=tuple(jax.ShapeDtypeStruct(r.shape, r.dtype) for r in results),
        in_specs=[pl.BlockSpec(memory_space=pl.ANY)] * 4,
        out_specs=(pl.BlockSpec(memory_space=pl.ANY),) * 4,
        scratch_shapes=[pltpu.VMEM(r.shape, r.dtype) for r in results]
        + [pltpu.SemaphoreType.DMA((2, 4))],
        compiler_params=pltpu.CompilerParams(vmem_limit_bytes=VMEM_BYTES),
        name="emit",
    )(*results)


def solution(mesh):
    return jax.shard_map(
        per_device,
        mesh=mesh,
        in_specs=(
            P("seq", "head"),
            P("seq", "head"),
            P("seq", "head"),
            P(),
            P(),
            P("seq", None),
            P("head", None),
        ),
        out_specs=(P("seq", "head"), P("seq", "head"), P("seq", "head"), P("seq", "head")),
        check_vma=False,
    )
```

time: 97 us -> 75.2 us (0.78)
  Pallas kernels: 86.2 us -> 74.4 us
  local copies, waits for them, and re-layouts: 9.86 us -> 0 us
    pallas_call x1, Pallas kernels: 86.2 us -> 72.6 us  [per_device(): pl.pallas_call(kernel, out_shape=(jax.ShapeDtypeStruct((HALF, 512), BF16)...]
    unnamed x18 -> x0, local copies, waits for them, and re-layouts: 9.86 us -> none
    pallas_call x0 -> x1, Pallas kernels: none -> 1.85 us  [per_device(): pl.pallas_call(emit, out_shape=tuple((jax.ShapeDtypeStruct(r.shape, r.dty...]
where the time goes in v2:
time: 75.2 us; the launch traced here: 75.1 us
  Pallas kernels  74.4 us (99%)
    pallas_call x1, Pallas kernels, per_device(): pl.pallas_call(kernel, out_shape=(jax.ShapeDtypeStruct((HALF, 512), BF16)...  72.6 us
    pallas_call x1, Pallas kernels, per_device(): pl.pallas_call(emit, out_shape=tuple((jax.ShapeDtypeStruct(r.shape, r.dty...  1.85 us

profile of v2, /device:TPU:1, one launch (start us, length us, event | category | flops | bytes accessed | tf_op | source)
XLA Modules:
  0.0 75.1 jit_solution(4690554009059103484)
XLA Ops:
  0.6 72.6 %attention_grads.1 = (bf16[256,512]{1,0:T(8,128)(2,1)}, bf16[256,256]{1,0:T(8,128)(2,1)}, bf16[256,256]{1,0:T(8,128)(2,1)}, bf16[256,256]{1,0:T(8,128)(2,1)}) custom-call(s32[64]{0:T(128)} %order_hbm.1, s32[8]{0:T(128)} %lengths_hbm.1, bf16[256,256]{1,0:T(8,128)(2,1)} %q_hbm.1, bf16[256,256]{1,0:T(8,128)(2,1)} %k_hbm.1, bf16[256,256]{1,0:T(8,128)(2,1)} %v_hbm.1, ...), custom_call_target="tpu_custom_call" | custom-call | tf_op jit(solution)/shard_map/attention_grads/pallas_call | solution.py:516
  73.2 1.8 %emit.1 = (bf16[256,512]{1,0:T(8,128)(2,1)}, bf16[256,256]{1,0:T(8,128)(2,1)}, bf16[256,256]{1,0:T(8,128)(2,1)}, bf16[256,256]{1,0:T(8,128)(2,1)}) custom-call(bf16[256,512]{1,0:T(8,128)(2,1)} %get-tuple-element.8.a, bf16[256,256]{1,0:T(8,128)(2,1)} %get-tuple-element.9.b, bf16[256,256]{1,0:T(8,128)(2,1)} %get-tuple-element.10.c, ...), custom_call_target="tpu_custom_call" | custom-call | tf_op jit(solution)/shard_map/emit/pallas_call | solution.py:563

commit v3 on v2

--- a/solution.py
+++ b/solution.py
@@ -62,8 +62,11 @@
     def seq_dev(t):
         return (t, k)
 
-    def head_dev(e):
-        return (s, (k + e) % NK)
+    def row_dev(e):
+        return (s, k - k % 4 + (k + e) % 4)
+
+    k_far = (k + 4) % NK
+    far_dev = (s, k_far)
 
     def weight_dev(e):
         kk = (k + e) % NK
@@ -72,8 +75,8 @@
 
     barrier = pltpu.get_barrier_semaphore()
     targets = [seq_dev(sibling), seq_dev(partner), seq_dev(diagonal)]
-    targets += [seq_dev(z_peer(e)) for e in range(1, NZ)]
-    targets += [head_dev(e) for e in range(1, NK)]
+    targets += [seq_dev(z_peer(e)) for e in (1, NZ - 1)]
+    targets += [row_dev(e) for e in range(1, 4)] + [far_dev]
     targets += [weight_dev(e) for e in range(1, NK)]
     for t in targets:
         pl.semaphore_signal(barrier, inc=1, device_id=t, device_id_type=MESH)
@@ -229,6 +232,7 @@
     ring_start(VALUES, 1)
     pair_k = to_pair(k_in, xk)
     pair_v = to_pair(v_in, xv)
+    ring_service(KEYS, 1)
 
     col_half = pl.ds(pl.multiple_of(core * 256, 256), 256)
     w_copies = []
@@ -244,7 +248,9 @@
 
     copy_l = plan(st_send.at[0], st_recv, seq_dev(partner))
     copy_o = plan(o_send, o_recv, seq_dev(partner))
-    att_copies = [plan(attg.at[k], attg.at[k], head_dev(e)) for e in range(1, NK)]
+    att_far = plan(attg.at[k], attg.at[k], far_dev)
+    att_near = [plan(attg.at[k], attg.at[k], row_dev(e)) for e in range(1, 4)]
+    att_relay = [plan(attg.at[k_far], attg.at[k_far], row_dev(e)) for e in range(1, 4)]
     grads = [
         [
             plan(grad_send.at[n, m], grad_recv.at[n, m], seq_dev(t))
@@ -256,8 +262,8 @@
     def block_rows(d):
         return pl.ds(pl.multiple_of((1 + d) * BLK, BLK), BLK)
 
-    def pair_of(p):
-        return ((NZ - p) % NZ, p + 1)
+    def block_of(i):
+        return jnp.where(i % 2 == 1, (i + 1) // 2, (NZ - i // 2) % NZ)
 
     own, theirs = pl.ds(BLK, BLK), pl.ds(0, BLK)
 
@@ -305,24 +311,22 @@
         totals = jnp.broadcast_to(totals, (BLK, HD))
         return o_acc[rows, :] / totals, m_acc[rows, :] + jnp.log(totals) * LOG2E
 
+    ring_service(VALUES, 1)
     for c in (sib_q, sib_g) + pair_q + pair_g:
         c.wait_recv()
-    ring_service(KEYS, 1)
 
     def forward_step(n, _):
-        p = n // 2
-
-        @pl.when(n < 7)
-        def _():
-            ring_service(1 - n % 2, (n + 1) // 2 + 1)
-
-        @pl.when(n == 4)
+        @pl.when((n % 2 == 0) & (n >= 4))
+        def _():
+            ring_service((n // 2) % 2, n // 4 + 1)
+
+        @pl.when(n == 10)
         def _():
             for a in (QUERIES, GRADS):
                 for j in (0, 1):
                     ring_start(a, j)
 
-        @pl.when(n == 7)
+        @pl.when(n == 15)
         def _():
             o_part, lse_part = close(theirs)
             o_send[...] = o_part.astype(BF16)
@@ -330,10 +334,10 @@
             copy_l.start()
             copy_o.start()
 
-        forward(pair_of(p), pl.ds(pl.multiple_of((n % 2) * BLK, BLK), BLK))
+        forward((block_of(n // 2),), pl.ds(pl.multiple_of((n % 2) * BLK, BLK), BLK))
         return 0
 
-    lax.fori_loop(0, 8, forward_step, 0)
+    lax.fori_loop(0, 16, forward_step, 0)
     ring_service(QUERIES, 1)
     o_own, lse_own = close(own)
     ring_service(GRADS, 1)
@@ -355,15 +359,25 @@
     delta = jnp.broadcast_to(delta, (BLK, HD))
     row8 = lax.broadcasted_iota(jnp.int32, (8, BLK), 0)
     st_z[0, :, :] = jnp.where(row8 == 0, lse.T[0:8, :], delta.T[0:8, :])
-    def stats_copy(e):
+    def stats_copy(back, t):
+        src, dst = ((9 - t) % NZ, NZ - t) if back else (t - 1, t)
         return pltpu.make_async_remote_copy(
-            src_ref=st_z.at[0], dst_ref=st_z.at[e],
-            send_sem=stat_send_sem.at[e], recv_sem=stat_recv_sem.at[e],
-            device_id=seq_dev(z_peer(e)), device_id_type=MESH,
+            src_ref=st_z.at[src], dst_ref=st_z.at[dst],
+            send_sem=stat_send_sem.at[back, t - 1], recv_sem=stat_recv_sem.at[back, t - 1],
+            device_id=seq_dev(z_peer(NZ - 1 if back else 1)), device_id_type=MESH,
         )
 
-    for e in (1, 7, 2, 6, 3, 5, 4):
-        stats_copy(e).start()
+    def stats_service(t):
+        stats_copy(0, t).wait_recv()
+        stats_copy(0, t + 1).start()
+        stats_copy(1, t).wait_recv()
+
+        @pl.when(t < 3)
+        def _():
+            stats_copy(1, t + 1).start()
+
+    for back in (0, 1):
+        stats_copy(back, 1).start()
     copy_sp = remote(st_z.at[0], st_par, seq_dev(partner))
     copy_a = remote(
         att.at[pl.ds(half_rows[1], HALF), :], attg.at[k, :, own_cols], seq_dev(sibling)
@@ -417,54 +431,71 @@
     for c in pair_k + pair_v:
         c.wait_recv()
 
-    def key_step(n, _):
-        p = n // 2
-
-        @pl.when(n > 0)
-        def _():
-            @pl.when(n < 7)
-            def _():
-                ring_service(3 - n % 2, (n + 1) // 2 + 1)
-
-        @pl.when(n % 2 == 0)
-        def _():
-            stats_copy(p + 1).wait_recv()
-
-            @pl.when(p > 0)
-            def _():
-                stats_copy(NZ - p).wait_recv()
-
-        @pl.when(n == 1)
+    def key_step(i, _):
+        @pl.when((i == 1) | (i == 4))
+        def _():
+            ring_service(QUERIES, i // 3 + 2)
+
+        @pl.when((i == 2) | (i == 5))
+        def _():
+            ring_service(GRADS, i // 3 + 2)
+
+        @pl.when(i == 6)
+        def _():
+            ring_service(QUERIES, 4)
+
+        @pl.when(i % 2 == 1)
+        def _():
+            stats_service((i + 1) // 2)
+
+        @pl.when(i == 1)
         def _():
             copy_a.wait_recv()
-            for c in att_copies:
+            for c in [att_far] + att_near:
                 c.start()
+
+        @pl.when(i == 2)
+        def _():
             copy_sp.wait_recv()
             close_queries(theirs, to_col(st_par[0:1, :]), to_col(st_par[1:2, :]))
             for m in (1, 2, 0):
                 send_grad(0, dq_acc, 1.0, m)
 
-        @pl.when(n == 2)
+        @pl.when(i == 3)
         def _():
             for c, d in zip(w_copies, w_sib):
                 c.wait_recv()
                 d.start()
 
-        @pl.when(n == 7)
+        @pl.when(i == 5)
+        def _():
+            att_far.wait_recv()
+            for c in att_relay:
+                c.start()
+
+        key_side((block_of(i),), pl.ds(0, PAIR))
+        return 0
+
+    lax.fori_loop(0, 7, key_step, 0)
+    ring_service(GRADS, 4)
+    stats_copy(0, 4).wait_recv()
+
+    def last_step(i, _):
+        @pl.when(i == 1)
         def _():
             for m in (1, 2):
                 send_grad(2, dv_acc, 1.0, m)
                 send_grad(1, dk_acc, SCALE, m)
 
-        key_side(pair_of(p), pl.ds(pl.multiple_of((n % 2) * BLK, BLK), BLK))
+        key_side((4,), pl.ds(pl.multiple_of(i * BLK, BLK), BLK))
         return 0
 
-    lax.fori_loop(0, 8, key_step, 0)
+    lax.fori_loop(0, 2, last_step, 0)
     send_grad(2, dv_acc, 1.0, 0)
     send_grad(1, dk_acc, SCALE, 0)
     stores = [finish_grad(0, dq_acc, 1.0, dq_hbm)]
 
-    for c in att_copies + w_sib:
+    for c in att_near + att_relay + w_sib:
         c.wait_recv()
 
     def project(i, total):
@@ -478,8 +509,10 @@
         c.wait()
     for c in pending:
         c.wait_send()
-    for e in range(1, NZ):
-        stats_copy(e).wait_send()
+    for t in range(1, 5):
+        stats_copy(0, t).wait_send()
+    for t in range(1, 4):
+        stats_copy(1, t).wait_send()
 
     def drain(a, _):
         for j in (0, 1):
@@ -551,8 +584,8 @@
             pltpu.SemaphoreType.DMA((COPIES,)),
             pltpu.SemaphoreType.DMA((4, 2, 4, 2)),
             pltpu.SemaphoreType.DMA((4, 2, 4, 2)),
-            pltpu.SemaphoreType.DMA((NZ,)),
-            pltpu.SemaphoreType.DMA((NZ,)),
+            pltpu.SemaphoreType.DMA((2, 4)),
+            pltpu.SemaphoreType.DMA((2, 4)),
             pltpu.SemaphoreType.DMA((11,)),
         ],
         compiler_params=pltpu.CompilerParams(

time: 75.2 us -> 70.7 us (0.940)
  Pallas kernels: 74.4 us -> 70 us
    pallas_call x1, Pallas kernels: 72.6 us -> 68.1 us  [per_device(): pl.pallas_call(kernel, out_shape=(jax.ShapeDtypeStruct((HALF, 512), BF16)...]
where the time goes in v3:
time: 70.7 us; the launch traced here: 70.6 us
  Pallas kernels  70 us (99%)
    pallas_call x1, Pallas kernels, per_device(): pl.pallas_call(kernel, out_shape=(jax.ShapeDtypeStruct((HALF, 512), BF16)...  68.1 us
    pallas_call x1, Pallas kernels, per_device(): pl.pallas_call(emit, out_shape=tuple((jax.ShapeDtypeStruct(r.shape, r.dty...  1.85 us

profile of v3, /device:TPU:1, one launch (start us, length us, event | category | flops | bytes accessed | tf_op | source)
XLA Modules:
  0.0 70.6 jit_solution(11386354868581253610)
XLA Ops:
  0.6 68.1 %attention_grads.1 = (bf16[256,512]{1,0:T(8,128)(2,1)}, bf16[256,256]{1,0:T(8,128)(2,1)}, bf16[256,256]{1,0:T(8,128)(2,1)}, bf16[256,256]{1,0:T(8,128)(2,1)}) custom-call(s32[64]{0:T(128)} %order_hbm.1, s32[8]{0:T(128)} %lengths_hbm.1, bf16[256,256]{1,0:T(8,128)(2,1)} %q_hbm.1, bf16[256,256]{1,0:T(8,128)(2,1)} %k_hbm.1, bf16[256,256]{1,0:T(8,128)(2,1)} %v_hbm.1, ...), custom_call_target="tpu_custom_call" | custom-call | tf_op jit(solution)/shard_map/attention_grads/pallas_call | solution.py:549
  68.8 1.8 %emit.1 = (bf16[256,512]{1,0:T(8,128)(2,1)}, bf16[256,256]{1,0:T(8,128)(2,1)}, bf16[256,256]{1,0:T(8,128)(2,1)}, bf16[256,256]{1,0:T(8,128)(2,1)}) custom-call(bf16[256,512]{1,0:T(8,128)(2,1)} %get-tuple-element.8.a, bf16[256,256]{1,0:T(8,128)(2,1)} %get-tuple-element.9.b, bf16[256,256]{1,0:T(8,128)(2,1)} %get-tuple-element.10.c, ...), custom_call_target="tpu_custom_call" | custom-call | tf_op jit(solution)/shard_map/emit/pallas_call | solution.py:596

commit v4 on v3

--- a/solution.py
+++ b/solution.py
@@ -89,8 +89,8 @@
     loads = [
         local(src, dst, n)
         for n, (src, dst) in enumerate((
-            (order_hbm, order), (lengths_hbm, lengths),
-            (k_hbm, k_in), (v_hbm, v_in), (q_hbm, q_in), (w_hbm, wfull), (og_hbm, og),
+            (k_hbm, k_in), (v_hbm, v_in), (q_hbm, q_in),
+            (order_hbm, order), (lengths_hbm, lengths), (w_hbm, wfull), (og_hbm, og),
         ))
     ]
 
@@ -102,7 +102,101 @@
     def rows_of(block, j):
         return pl.ds(pl.multiple_of(block * BLK + half_rows[j], HALF), HALF)
 
-    for c in loads[:2]:
+    own_rows = rows_of(1, 0)
+    for c in loads[:3]:
+        c.wait()
+    xk[own_rows, :] = k_in[:, own_cols]
+    xv[own_rows, :] = v_in[:, own_cols]
+    xq[own_rows, :] = q_in[:, own_cols]
+    pl.semaphore_wait(barrier, len(targets))
+
+    counter = [0]
+    pending = []
+
+    def plan(src, dst, target):
+        n = counter[0]
+        counter[0] += 1
+        copy = pltpu.make_async_remote_copy(
+            src_ref=src, dst_ref=dst, send_sem=send_sem.at[n], recv_sem=recv_sem.at[n],
+            device_id=target, device_id_type=MESH,
+        )
+        pending.append(copy)
+        return copy
+
+    def remote(src, dst, target):
+        copy = plan(src, dst, target)
+        copy.start()
+        return copy
+
+    def ring_copy(a, back, t, j):
+        src, dst = (1 + (9 - t) % NZ, 9 - t) if back else (t, 1 + t)
+        return pltpu.make_async_remote_copy(
+            src_ref=xa.at[a, rows_of(src, j), :], dst_ref=xa.at[a, rows_of(dst, j), :],
+            send_sem=ring_send_sem.at[a, back, t - 1, j],
+            recv_sem=ring_recv_sem.at[a, back, t - 1, j],
+            device_id=seq_dev(z_peer(NZ - 1 if back else 1)), device_id_type=MESH,
+        )
+
+    def ring_start(a, j):
+        for back in (0, 1):
+            ring_copy(a, back, 1, j).start()
+
+    def ring_service(a, t):
+        for j in (0, 1):
+            for back in (0, 1):
+                if j == back:
+                    ring_copy(a, back, t, j).wait_recv()
+
+                    @pl.when(t < 4)
+                    def _():
+                        ring_copy(a, back, t + 1, j).start()
+                else:
+                    @pl.when(t < 4)
+                    def _():
+                        ring_copy(a, back, t, j).wait_recv()
+
+                    @pl.when(t < 3)
+                    def _():
+                        ring_copy(a, back, t + 1, j).start()
+
+    def to_sibling(src, arr):
+        return remote(src.at[:, other_cols], arr.at[rows_of(1, 0), :], seq_dev(sibling))
+
+    def to_pair(src, arr):
+        return (
+            remote(src.at[:, own_cols], arr.at[rows_of(0, 0), :], seq_dev(partner)),
+            remote(src.at[:, other_cols], arr.at[rows_of(0, 0), :], seq_dev(diagonal)),
+        )
+
+    sib_k = to_sibling(k_in, xk)
+    sib_v = to_sibling(v_in, xv)
+    ring_start(KEYS, 0)
+    ring_start(VALUES, 0)
+    sib_q = to_sibling(q_in, xq)
+    pair_q = to_pair(q_in, xq)
+    sib_k.wait_recv()
+    ring_start(KEYS, 1)
+    sib_v.wait_recv()
+    ring_start(VALUES, 1)
+
+    for c in loads[5:]:
+        c.wait()
+    da_acc[...] = jnp.zeros((HALF, HALF), F32)
+
+    def da_body(i, _):
+        cols = pl.ds(pl.multiple_of(i * 1024, 1024), 1024)
+        da_acc[...] += dot_nt(og[:, cols], wfull[:, cols])
+        return 0
+
+    lax.fori_loop(0, 4, da_body, 0)
+    da[...] = da_acc[...].astype(BF16)
+    xg[own_rows, :] = da[:, own_cols]
+    sib_g = to_sibling(da, xg)
+    pair_g = to_pair(da, xg)
+    pair_k = to_pair(k_in, xk)
+    pair_v = to_pair(v_in, xv)
+
+    for c in loads[3:5]:
         c.wait()
     ends = []
     total = jnp.int32(0)
@@ -135,103 +229,10 @@
     def base(d, j):
         return order[chip_group((z + NZ - d) % NZ, x) + j] * GROUP
 
-    own_rows = rows_of(1, 0)
-    for c in loads[2:5]:
-        c.wait()
-    xk[own_rows, :] = k_in[:, own_cols]
-    xv[own_rows, :] = v_in[:, own_cols]
-    xq[own_rows, :] = q_in[:, own_cols]
     m_acc[...] = jnp.full((PAIR, HD), LOWEST, F32)
     for acc in (l_acc, o_acc, a1_acc, a2_acc, dk_acc, dv_acc):
         acc[...] = jnp.zeros((PAIR, HD), F32)
 
-    for c in loads[5:]:
-        c.wait()
-    da_acc[...] = jnp.zeros((HALF, HALF), F32)
-
-    def da_body(i, _):
-        cols = pl.ds(pl.multiple_of(i * 1024, 1024), 1024)
-        da_acc[...] += dot_nt(og[:, cols], wfull[:, cols])
-        return 0
-
-    lax.fori_loop(0, 4, da_body, 0)
-    da[...] = da_acc[...].astype(BF16)
-    xg[own_rows, :] = da[:, own_cols]
-
-    pl.semaphore_wait(barrier, len(targets))
-
-    counter = [0]
-    pending = []
-
-    def plan(src, dst, target):
-        n = counter[0]
-        counter[0] += 1
-        copy = pltpu.make_async_remote_copy(
-            src_ref=src, dst_ref=dst, send_sem=send_sem.at[n], recv_sem=recv_sem.at[n],
-            device_id=target, device_id_type=MESH,
-        )
-        pending.append(copy)
-        return copy
-
-    def remote(src, dst, target):
-        copy = plan(src, dst, target)
-        copy.start()
-        return copy
-
-    def ring_copy(a, back, t, j):
-        src, dst = (1 + (9 - t) % NZ, 9 - t) if back else (t, 1 + t)
-        return pltpu.make_async_remote_copy(
-            src_ref=xa.at[a, rows_of(src, j), :], dst_ref=xa.at[a, rows_of(dst, j), :],
-            send_sem=ring_send_sem.at[a, back, t - 1, j],
-            recv_sem=ring_recv_sem.at[a, back, t - 1, j],
-            device_id=seq_dev(z_peer(NZ - 1 if back else 1)), device_id_type=MESH,
-        )
-
-    def ring_start(a, j):
-        for back in (0, 1):
-            ring_copy(a, back, 1, j).start()
-
-    def ring_service(a, t):
-        for j in (0, 1):
-            for back in (0, 1):
-                if j == back:
-                    ring_copy(a, back, t, j).wait_recv()
-
-                    @pl.when(t < 4)
-                    def _():
-                        ring_copy(a, back, t + 1, j).start()
-                else:
-                    @pl.when(t < 4)
-                    def _():
-                        ring_copy(a, back, t, j).wait_recv()
-
-                    @pl.when(t < 3)
-                    def _():
-                        ring_copy(a, back, t + 1, j).start()
-
-    def to_sibling(src, arr):
-        return remote(src.at[:, other_cols], arr.at[rows_of(1, 0), :], seq_dev(sibling))
-
-    def to_pair(src, arr):
-        return (
-            remote(src.at[:, own_cols], arr.at[rows_of(0, 0), :], seq_dev(partner)),
-            remote(src.at[:, other_cols], arr.at[rows_of(0, 0), :], seq_dev(diagonal)),
-        )
-
-    sib_k = to_sibling(k_in, xk)
-    sib_v = to_sibling(v_in, xv)
-    ring_start(KEYS, 0)
-    ring_start(VALUES, 0)
-    sib_q = to_sibling(q_in, xq)
-    sib_g = to_sibling(da, xg)
-    pair_q = to_pair(q_in, xq)
-    pair_g = to_pair(da, xg)
-    sib_k.wait_recv()
-    ring_start(KEYS, 1)
-    sib_v.wait_recv()
-    ring_start(VALUES, 1)
-    pair_k = to_pair(k_in, xk)
-    pair_v = to_pair(v_in, xv)
     ring_service(KEYS, 1)
 
     col_half = pl.ds(pl.multiple_of(core * 256, 256), 256)

time: 70.7 us -> 68.5 us (0.969)
  Pallas kernels: 70 us -> 67.8 us
    pallas_call x1, Pallas kernels: 68.1 us -> 65.9 us  [per_device(): pl.pallas_call(kernel, out_shape=(jax.ShapeDtypeStruct((HALF, 512), BF16)...]
where the time goes in v4:
time: 68.5 us; the launch traced here: 68.4 us
  Pallas kernels  67.8 us (99%)
    pallas_call x1, Pallas kernels, per_device(): pl.pallas_call(kernel, out_shape=(jax.ShapeDtypeStruct((HALF, 512), BF16)...  65.9 us
    pallas_call x1, Pallas kernels, per_device(): pl.pallas_call(emit, out_shape=tuple((jax.ShapeDtypeStruct(r.shape, r.dty...  1.85 us

profile of v4, /device:TPU:1, one launch (start us, length us, event | category | flops | bytes accessed | tf_op | source)
XLA Modules:
  0.0 68.4 jit_solution(2960340150252638557)
XLA Ops:
  0.6 65.9 %attention_grads.1 = (bf16[256,512]{1,0:T(8,128)(2,1)}, bf16[256,256]{1,0:T(8,128)(2,1)}, bf16[256,256]{1,0:T(8,128)(2,1)}, bf16[256,256]{1,0:T(8,128)(2,1)}) custom-call(s32[64]{0:T(128)} %order_hbm.1, s32[8]{0:T(128)} %lengths_hbm.1, bf16[256,256]{1,0:T(8,128)(2,1)} %q_hbm.1, bf16[256,256]{1,0:T(8,128)(2,1)} %k_hbm.1, bf16[256,256]{1,0:T(8,128)(2,1)} %v_hbm.1, ...), custom_call_target="tpu_custom_call" | custom-call | tf_op jit(solution)/shard_map/attention_grads/pallas_call | solution.py:550
  66.6 1.8 %emit.1 = (bf16[256,512]{1,0:T(8,128)(2,1)}, bf16[256,256]{1,0:T(8,128)(2,1)}, bf16[256,256]{1,0:T(8,128)(2,1)}, bf16[256,256]{1,0:T(8,128)(2,1)}) custom-call(bf16[256,512]{1,0:T(8,128)(2,1)} %get-tuple-element.8.a, bf16[256,256]{1,0:T(8,128)(2,1)} %get-tuple-element.9.b, bf16[256,256]{1,0:T(8,128)(2,1)} %get-tuple-element.10.c, ...), custom_call_target="tpu_custom_call" | custom-call | tf_op jit(solution)/shard_map/emit/pallas_call | solution.py:597

commit v5 on v4

--- a/solution.py
+++ b/solution.py
@@ -168,9 +168,9 @@
             remote(src.at[:, other_cols], arr.at[rows_of(0, 0), :], seq_dev(diagonal)),
         )
 
+    ring_start(KEYS, 0)
     sib_k = to_sibling(k_in, xk)
     sib_v = to_sibling(v_in, xv)
-    ring_start(KEYS, 0)
     ring_start(VALUES, 0)
     sib_q = to_sibling(q_in, xq)
     pair_q = to_pair(q_in, xq)
@@ -321,11 +321,15 @@
         def _():
             ring_service((n // 2) % 2, n // 4 + 1)
 
+        @pl.when(n == 8)
+        def _():
+            ring_start(QUERIES, 0)
+
         @pl.when(n == 10)
         def _():
-            for a in (QUERIES, GRADS):
-                for j in (0, 1):
-                    ring_start(a, j)
+            ring_start(QUERIES, 1)
+            for j in (0, 1):
+                ring_start(GRADS, j)
 
         @pl.when(n == 15)
         def _():

time: 68.5 us -> 68.6 us (level)
  no operation moved by 1% of the time
where the time goes in v5:
time: 68.6 us; the launch traced here: 68.5 us
  Pallas kernels  67.8 us (99%)
    pallas_call x1, Pallas kernels, per_device(): pl.pallas_call(kernel, out_shape=(jax.ShapeDtypeStruct((HALF, 512), BF16)...  66 us
    pallas_call x1, Pallas kernels, per_device(): pl.pallas_call(emit, out_shape=tuple((jax.ShapeDtypeStruct(r.shape, r.dty...  1.85 us

profile of v5, /device:TPU:1, one launch (start us, length us, event | category | flops | bytes accessed | tf_op | source)
XLA Modules:
  0.0 68.5 jit_solution(7205905382860004778)
XLA Ops:
  0.6 66.0 %attention_grads.1 = (bf16[256,512]{1,0:T(8,128)(2,1)}, bf16[256,256]{1,0:T(8,128)(2,1)}, bf16[256,256]{1,0:T(8,128)(2,1)}, bf16[256,256]{1,0:T(8,128)(2,1)}) custom-call(s32[64]{0:T(128)} %order_hbm.1, s32[8]{0:T(128)} %lengths_hbm.1, bf16[256,256]{1,0:T(8,128)(2,1)} %q_hbm.1, bf16[256,256]{1,0:T(8,128)(2,1)} %k_hbm.1, bf16[256,256]{1,0:T(8,128)(2,1)} %v_hbm.1, ...), custom_call_target="tpu_custom_call" | custom-call | tf_op jit(solution)/shard_map/attention_grads/pallas_call | solution.py:554
  66.6 1.8 %emit.1 = (bf16[256,512]{1,0:T(8,128)(2,1)}, bf16[256,256]{1,0:T(8,128)(2,1)}, bf16[256,256]{1,0:T(8,128)(2,1)}, bf16[256,256]{1,0:T(8,128)(2,1)}) custom-call(bf16[256,512]{1,0:T(8,128)(2,1)} %get-tuple-element.8.a, bf16[256,256]{1,0:T(8,128)(2,1)} %get-tuple-element.9.b, bf16[256,256]{1,0:T(8,128)(2,1)} %get-tuple-element.10.c, ...), custom_call_target="tpu_custom_call" | custom-call | tf_op jit(solution)/shard_map/emit/pallas_call | solution.py:601
